TPU v7x, 32 devices: a whole 2x2x4 slice. The times are simulated.
32 devices in a mesh: parts: 2 (over x), xy: 16 (over z, y, core).
Axes of the slice: x: 2, y: 2, z: 4, core: 2. Of those that a mesh axis runs over, the one named last changes fastest.
Arguments:
- affinity: bfloat16 [3, 256, 64, 128], P(None, ('parts', 'xy')), parts along dimension 1, may hold values from 0 to 1
- block_scale: float32 [3, 256, 64], P(None, ('parts', 'xy')), parts along dimension 1, may hold values from 0.5 to 2
- slot_map: int32 [256, 64, 128], P(('parts', 'xy')), parts along dimension 0, may hold values from 0 to 7, as said below
- edge_list: int32 [256, 64, 8], P(('parts', 'xy')), parts along dimension 0, may hold values from 0 to 8191, as said below
- valid_count: int32 [256, 64], P(('parts', 'xy')), parts along dimension 0, may hold values from 5 to 8
- edge_home: int32 [16384], P('parts'), parts along dimension 0, may hold values from 0 to 8191, as said below
Outputs:
- edge_features: float32 [16384, 64], P(('parts', 'xy')), parts along dimension 0
There are 2 independent parts, one for each index of `parts`. A program takes and returns all parts, laid end to end along the dimension named above; each array names one. Nothing has to cross between parts.
Inputs may be any that keep to these rules, and one draw needn't show every extreme that they name: `slot_map`: every voxel's entry is below its block's valid_count. `edge_list`: among the used entries of the blocks of one device (8 planes), at most 512 name edges whose edge_home lies in any one range [k * 512, (k + 1) * 512); in every draw some range receives exactly 512 from every device. `edge_home`: a permutation of 0 to 8191.
All inputs are finite; a program needn't handle non-finite values.
Results may differ from a plain program's by a relative error of at most 0.0003.
Values sent between devices are 32-bit elements; how exact they have to be, the bound alone decides.
A program may use at most 64 MiB of HBM per device.

v0:
```python
import functools
import math
import ml_dtypes
import numpy as np
import jax
import jax.numpy as jnp
from jax import lax
from jax.experimental import pallas as pl
from jax.experimental.pallas import tpu as pltpu
from jax.sharding import PartitionSpec as P

SLOTS = 8
HALO = 8
FEAT = 64
SIGMAS = (0.8, 1.3, 2.0, 3.0)
MESH = pl.DeviceIdType.MESH
VMEM = pltpu.VMEM


def taps(sigma):
    t = np.arange(-HALO, HALO + 1).astype(np.float64)
    w = np.exp(-t * t / (2.0 * sigma * sigma))
    return (w / w.sum()).astype(np.float32)


def band(sigma, length):
    w = taps(sigma)
    rows = np.arange(length)
    shift = rows[None, :] - rows[:, None] + HALO
    inside = (shift >= 0) & (shift <= 2 * HALO)
    full = np.where(inside, w[np.clip(shift, 0, 2 * HALO)], np.float32(0)).astype(np.float32)
    high = full.astype(ml_dtypes.bfloat16)
    low = (full - high.astype(np.float32)).astype(ml_dtypes.bfloat16)
    return high, low


def split(value):
    high = value.astype(jnp.bfloat16)
    low = (value - high.astype(jnp.float32)).astype(jnp.bfloat16)
    return high, low


def bits_of(n):
    return [1 << k for k in range(n.bit_length() - 1)]


def orders(n):
    bits = bits_of(n)
    return (bits, bits[:1] + bits[2:] + bits[1:2])


def rank_of(dest, order):
    rank = jnp.zeros_like(dest)
    for bit in order:
        rank = rank * 2 + (dest // bit) % 2
    return rank


def sums_kernel(edges, banks, before, own, after, slots, along_y, along_z, elist, place, out, ext, resp, prod, rows, *tables):
    q = pl.program_id(0)
    planes, height, depth = own.shape[1:]

    @pl.when(q == 0)
    def _():
        ext[:, :HALO] = before[...]
        ext[:, HALO:HALO + planes] = own[...]
        ext[:, HALO + planes:] = after[...]
        for table in tables:
            @pl.loop(0, table.shape[0] // 64)
            def _(r):
                table[pl.ds(pl.multiple_of(r * 64, 64), 64), :] = jnp.zeros((64, 128), jnp.float32)

    weights = [taps(s) for s in SIGMAS]
    crossed = [[] for _ in SIGMAS]
    for c in range(3):
        chunks = [[] for _ in SIGMAS]
        for z in range(0, height, 16):
            mid = ext[c, q + HALO, z:z + 16, :]
            acc = [mid * float(w[HALO]) for w in weights]
            for t in range(1, HALO + 1):
                both = ext[c, q + HALO - t, z:z + 16, :] + ext[c, q + HALO + t, z:z + 16, :]
                acc = [a + both * float(w[HALO + t]) for a, w in zip(acc, weights)]
            for i in range(4):
                chunks[i].append(acc[i])
        for i in range(4):
            crossed[i].append(jnp.concatenate(chunks[i], 0))
    for i in range(4):
        high, low = split(jnp.concatenate(crossed[i], 0))
        wide = jnp.dot(jnp.concatenate([high, low], 1), along_y[i], preferred_element_type=jnp.float32)
        field = wide[:, :depth] + wide[:, depth:]
        high, low = split(field)
        highs = jnp.concatenate([high[c * height:(c + 1) * height] for c in range(3)], 1)
        lows = jnp.concatenate([low[c * height:(c + 1) * height] for c in range(3)], 1)
        stacked = jnp.concatenate([highs, lows, highs, lows], 0)
        done = jnp.dot(along_z[i], stacked, preferred_element_type=jnp.float32)
        for c in range(3):
            resp[3 * i + c] = done[:, c * depth:(c + 1) * depth]

    slot_row = lax.broadcasted_iota(jnp.int32, (SLOTS, 128), 0)
    lane_z = lax.broadcasted_iota(jnp.int32, (8, 64), 1) // SLOTS

    @pl.loop(0, height // 16)
    def _(j):
        parts = []
        for g in range(2):
            z0 = pl.multiple_of(j * 16 + g * 8, 8)
            r = [resp[k, pl.ds(z0, 8), :] for k in range(12)]
            raw = [ext[c, q + HALO, pl.ds(z0, 8), :] for c in range(3)]
            square = [a * a for a in r]
            cube = [a * b for a, b in zip(square, r)]
            fourth = [a * a for a in square]
            pairs = []
            for i in range(4):
                a, b, c = r[3 * i:3 * i + 3]
                pairs += [a * b, a * c, b * c]
            ones = [jnp.ones((8, 128), jnp.float32)]
            feats = jnp.concatenate(r + square + cube + fourth + pairs + raw + ones, 0)
            high, low = split(feats)
            lhs = jnp.concatenate([high, low], 1)
            slot = slots[0, pl.ds(z0, 8), :]
            hot = jnp.concatenate([
                (jnp.broadcast_to(slot[k:k + 1, :], (SLOTS, 128)) == slot_row).astype(jnp.float32) for k in range(8)
            ], 0).astype(jnp.bfloat16)
            rhs = jnp.concatenate([hot, hot], 1)
            prod[g] = lax.dot_general(lhs, rhs, (((1,), (1,)), ((), ())), preferred_element_type=jnp.float32)
            pieces = []
            for f in range(0, FEAT, 8):
                piece = prod[g, pl.ds(f * 8, 8, stride=8), :]
                for k in range(1, 8):
                    piece = jnp.where(lane_z == k, prod[g, pl.ds(f * 8 + k, 8, stride=8), :], piece)
                pieces.append(piece)
            parts.append(jnp.concatenate(pieces, 0))
        block = jnp.concatenate(parts, 1)
        rows[...] = jnp.transpose(jnp.concatenate([block, jnp.zeros_like(block)], 0), (1, 0))
        base = q * (height * SLOTS) + j * 128

        @pl.loop(0, 128 // 8)
        def _(k8):
            for u in range(8):
                e = k8 * 8 + u
                at = place[elist[base + e]]
                table = tables[u % banks]
                table[pl.ds(at, 1), :] += rows[pl.ds(e, 1), :]

    @pl.when(q == pl.num_programs(0) - 1)
    def _():
        tile = out.shape[2]
        low_lane = lax.broadcasted_iota(jnp.int32, (tile, 128), 1) < FEAT

        @pl.loop(0, out.shape[0] * out.shape[1])
        def _(b):
            def total(start):
                at = pl.ds(pl.multiple_of(start, 8), tile)
                value = tables[0][at, :]
                for table in tables[1:]:
                    value = value + table[at, :]
                return value
            first = total(b * 2 * tile)
            second = total(b * 2 * tile + tile)
            second = pltpu.roll(second, FEAT, 1)
            out[b // out.shape[1], b % out.shape[1]] = jnp.where(low_lane, first, second)


def reduce_kernel(n, lists, table, out, *scratch):
    count = n.bit_length() - 1
    recv = scratch[:count]
    acc = scratch[count:2 * count]
    send_sem, recv_sem = scratch[2 * count:]
    me = lax.axis_index("xy")
    part_id = lax.axis_index("parts")

    def partner(bit):
        return me + bit * (1 - 2 * ((me // bit) % 2))

    barrier = pltpu.get_barrier_semaphore()
    for bit in bits_of(n):
        pl.semaphore_signal(barrier, inc=1, device_id=(part_id, partner(bit)), device_id_type=MESH)
    pl.semaphore_wait(barrier, count)

    copies = {}

    def start(p, k):
        bit = lists[p][k]
        size = n >> (k + 1)
        mine = (me // bit) % 2
        source = table.at[p] if k == 0 else acc[k - 1].at[p]
        copy = pltpu.make_async_remote_copy(
            src_ref=source.at[pl.ds((1 - mine) * size, size)],
            dst_ref=recv[k].at[p],
            send_sem=send_sem.at[p, k],
            recv_sem=recv_sem.at[p, k],
            device_id=(part_id, partner(bit)),
            device_id_type=MESH,
        )
        copy.start()
        copies[p, k] = copy

    def finish(p, k):
        bit = lists[p][k]
        size = n >> (k + 1)
        mine = (me // bit) % 2
        source = table.at[p] if k == 0 else acc[k - 1].at[p]
        copies[p, k].wait_recv()
        if k == count - 1:
            out[p] = source[mine] + recv[k][p, 0]
        else:
            acc[k][p] = source[pl.ds(mine * size, size)] + recv[k][p]

    for p in range(2):
        start(p, 0)
    for k in range(count):
        for p in range(2):
            finish(p, k)
            if k + 1 < count:
                start(p, k + 1)
    for copy in copies.values():
        copy.wait_send()


def finalize(table):
    count = table[:, FEAT - 1:]
    means = table[:, :FEAT - 1] / jnp.maximum(count, 1.0)
    return jnp.concatenate([means, jnp.log1p(count)], 1)


def shards(affinity, block_scale, slot_map, edge_list, valid_count, edge_home):
    planes, height, depth = affinity.shape[1:]
    n = lax.axis_size("xy")
    edges = edge_home.shape[0]
    e_dev = edges // n
    tile = e_dev // 4
    lists = orders(n)
    dequant = affinity.astype(jnp.float32) * block_scale[..., None]
    up = [(i, i + 1) for i in range(n - 1)]
    down = [(j, i) for i, j in up]
    before = lax.ppermute(dequant, "xy", up)
    after = lax.ppermute(dequant, "xy", down)

    dest, inner = edge_home // e_dev, edge_home % e_dev
    half, inner = inner // (2 * tile), inner % (2 * tile)
    part, row = inner // tile, inner % tile
    rank = jnp.where(part == 0, rank_of(dest, lists[0]), rank_of(dest, lists[1]))
    place = ((part * n + rank) * 2 + half) * tile + row
    place = jnp.concatenate([place, jnp.full((128,), edges, jnp.int32)])
    valid = jnp.arange(SLOTS, dtype=jnp.int32) < valid_count[..., None]
    elist = jnp.where(valid, edge_list, edges).reshape(-1)

    ys, zs = [], []
    for sigma in SIGMAS:
        high, low = band(sigma, depth)
        ys.append(np.block([[high, low], [high, low]]))
        high, low = band(sigma, height)
        zs.append(np.concatenate([high, high, low, low], 1))
    along_y = jnp.asarray(np.stack(ys), jnp.bfloat16)
    along_z = jnp.asarray(np.stack(zs), jnp.bfloat16)
    banks = 4 if edges * 512 * 4 <= (24 << 20) else 1
    whole = pl.BlockSpec(memory_space=VMEM)
    smem = pl.BlockSpec(memory_space=pltpu.SMEM)
    table = pl.pallas_call(
        functools.partial(sums_kernel, edges, banks),
        grid=(planes,),
        out_shape=jax.ShapeDtypeStruct((2, n, tile, 128), jnp.float32),
        in_specs=[whole, whole, whole, pl.BlockSpec((1, height, depth), lambda q: (q, 0, 0)), whole, whole, smem, smem],
        out_specs=whole,
        scratch_shapes=[
            VMEM((3, planes + 2 * HALO, height, depth), jnp.float32),
            VMEM((12, height, depth), jnp.float32),
            VMEM((2, FEAT * 8, 64), jnp.float32),
            VMEM((128, 128), jnp.float32),
        ] + [VMEM((edges + 64, 128), jnp.float32)] * banks,
        compiler_params=pltpu.CompilerParams(vmem_limit_bytes=56 << 20),
    )(before, dequant, after, slot_map, along_y, along_z, elist, place)

    count = n.bit_length() - 1
    sizes = [n >> (k + 1) for k in range(count)]
    total = pl.pallas_call(
        functools.partial(reduce_kernel, n, lists),
        out_shape=jax.ShapeDtypeStruct((2, tile, 128), jnp.float32),
        in_specs=[whole],
        out_specs=whole,
        scratch_shapes=[VMEM((2, s, tile, 128), jnp.float32) for s in sizes] * 2 + [
            pltpu.SemaphoreType.DMA((2, count)),
            pltpu.SemaphoreType.DMA((2, count)),
        ],
        compiler_params=pltpu.CompilerParams(collective_id=0, has_side_effects=True, vmem_limit_bytes=56 << 20),
    )(table)
    total = total.reshape(2 * tile, 128)
    return finalize(jnp.concatenate([total[:, :FEAT], total[:, FEAT:]], 0))


def solution(mesh):
    in_specs = (
        P(None, ("parts", "xy"), None, None),
        P(None, ("parts", "xy"), None),
        P(("parts", "xy"), None, None),
        P(("parts", "xy"), None, None),
        P(("parts", "xy"), None),
        P("parts"),
    )
    out_specs = P(("parts", "xy"), None)
    return jax.shard_map(shards, mesh=mesh, in_specs=in_specs, out_specs=out_specs, check_vma=False)
```

profile of v0, /device:TPU:0, one launch (start us, length us, event | category | flops | bytes accessed | tf_op | source)
XLA Modules:
  0.0 93.6 jit_solution(7360196845653350640)
XLA Ops:
  0.0 1.3 %convert_multiply_fusion.own = f32[3,8,64,128]{3,2,1,0:T(8,128)S(1)} fusion(bf16[3,8,64,128]{3,2,1,0:T(8,128)(2,1)} %param.8, f32[3,8,64]{2,1,0:T(8,128)} %param.9), kind=kLoop, calls=%fused_computation | loop fusion | flops 393216 | bytes 1185792 | tf_op jit(solution)/shard_map/mul | solution.py:233
  1.3 0.0 copy-start
  1.3 1.3 %collective-permute-start.1 = (f32[3,8,64,128]{3,2,1,0:T(8,128)S(1)}, f32[3,8,64,128]{3,2,1,0:T(8,128)S(1)}, u32[]{:S(2)}, u32[]{:S(2)}) collective-permute-start(f32[3,8,64,128]{3,2,1,0:T(8,128)S(1)} %convert_multiply_fusion.own), channel_id=1, source_target_pairs={{1,0},{2,1},{3,2},{4,3},{5,4},{6,5},{7,6},{8,7},{9,8},{10,9},{11,1... | collective-permute-start | bytes 2359304 | tf_op jit(solution)/shard_map/ppermute | solution.py:237
  2.6 3.1 %collective-permute-start = (f32[3,8,64,128]{3,2,1,0:T(8,128)S(1)}, f32[3,8,64,128]{3,2,1,0:T(8,128)S(1)}, u32[]{:S(2)}, u32[]{:S(2)}) collective-permute-start(f32[3,8,64,128]{3,2,1,0:T(8,128)S(1)} %convert_multiply_fusion.own), channel_id=1, source_target_pairs={{0,1},{1,2},{2,3},{3,4},{4,5},{5,6},{6,7},{7,8},{8,9},{9,10},{10,1... | collective-permute-start | bytes 2359304 | tf_op jit(solution)/shard_map/ppermute | solution.py:236
  5.7 0.8 fusion.9
  6.4 0.1 copy.11
  6.6 0.8 reshape.8.elist
  7.3 1.0 %fusion.8 = s32[8192]{0:T(1024)S(1)} fusion(s32[8192]{0:T(1024)} %param.13), kind=kLoop, calls=%fused_computation.46 | loop fusion | flops 1212416 | bytes 65536 | tf_op jit(solution)/shard_map/add | solution.py:243
  8.3 0.6 concatenate.9.place
  8.9 0.0 collective-permute-done.1.after
  8.9 0.0 copy-start.1
  8.9 0.0 collective-permute-done.before
  8.9 0.0 copy-done
  8.9 0.9 copy-done.1
  9.8 0.0 copy-start.2
  9.8 0.9 copy-done.2
  10.7 38.6 %shard_map.82.table = f32[2,16,128,128]{3,2,1,0:T(8,128)} custom-call(f32[3,8,64,128]{3,2,1,0:T(8,128)} %copy-done.2, f32[3,8,64,128]{3,2,1,0:T(8,128)} %copy-done, f32[3,8,64,128]{3,2,1,0:T(8,128)} %copy-done.1, s32[8,64,128]{2,1,0:T(8,128)} %slots.1, bf16[4,256,256]{2,1,0:T(8,128)(2,1)} %constant.163.clone.along_y, ...), custom_call_target="tpu_custom_call" | custom-call | tf_op jit(solution)/shard_map/pallas_call | solution.py:259
  49.3 42.3 %shard_map.83 = f32[2,128,128]{2,1,0:T(8,128)} custom-call(f32[2,16,128,128]{3,2,1,0:T(8,128)} %shard_map.82.table), custom_call_target="tpu_custom_call" | custom-call | tf_op jit(solution)/shard_map/pallas_call | solution.py:276
  91.6 1.1 %fusion.18 = (f32[256,64]{1,0:T(8,128)S(1)}, f32[256,64]{1,0:T(8,128)S(1)}) fusion(f32[256,128]{1,0:T(8,128)} %bitcast.2), kind=kLoop, calls=%fused_computation.63 | loop fusion | bytes 262144 | tf_op jit(solution)/shard_map/slice | solution.py:288
  92.7 0.1 copy.14
  92.8 0.1 copy.15
  93.0 0.7 pad_maximum_fusion
  (3 shorter events, 0.0 us)
Async XLA Ops:
  1.3 7.6 %copy-start = (f32[3,8,64,128]{3,2,1,0:T(8,128)}, f32[3,8,64,128]{3,2,1,0:T(8,128)S(1)}, u32[]{:S(2)}) copy-start(f32[3,8,64,128]{3,2,1,0:T(8,128)S(1)} %convert_multiply_fusion.own) | copy-start | bytes 2359300
  1.3 7.6 %collective-permute-start.1 = (f32[3,8,64,128]{3,2,1,0:T(8,128)S(1)}, f32[3,8,64,128]{3,2,1,0:T(8,128)S(1)}, u32[]{:S(2)}, u32[]{:S(2)}) collective-permute-start(f32[3,8,64,128]{3,2,1,0:T(8,128)S(1)} %convert_multiply_fusion.own), channel_id=1, source_target_pairs={{1,0},{2,1},{3,2},{4,3},{5,4},{6,5},{7,6},{8,7},{9,8},{10,9},{11,1... | collective-permute-start | bytes 2359304 | tf_op jit(solution)/shard_map/ppermute | solution.py:237
  2.6 6.3 %collective-permute-start = (f32[3,8,64,128]{3,2,1,0:T(8,128)S(1)}, f32[3,8,64,128]{3,2,1,0:T(8,128)S(1)}, u32[]{:S(2)}, u32[]{:S(2)}) collective-permute-start(f32[3,8,64,128]{3,2,1,0:T(8,128)S(1)} %convert_multiply_fusion.own), channel_id=1, source_target_pairs={{0,1},{1,2},{2,3},{3,4},{4,5},{5,6},{6,7},{7,8},{8,9},{9,10},{10,1... | collective-permute-start | bytes 2359304 | tf_op jit(solution)/shard_map/ppermute | solution.py:236
  8.9 0.9 copy-start.1
  9.8 0.9 copy-start.2
where the time goes:
time: 94 us; the launch traced here: 93.6 us
  Pallas kernels  81 us (86%)
  local copies, waits for them, and re-layouts  4.5 us (5%)
  starting transfers between devices  4.37 us (5%)
  other arithmetic  3.68 us (4%)
    pallas_call x1, Pallas kernels, shards(): pl.pallas_call(functools.partial(reduce_kernel, n, lists), out_shape=jax....  42.3 us
    pallas_call x1, Pallas kernels, shards(): pl.pallas_call(functools.partial(sums_kernel, edges, banks), grid=(planes...  38.6 us
    ppermute x1, starting transfers between devices, shards(): before = lax.ppermute(dequant, 'xy', up)  3.08 us
    unnamed x8, local copies, waits for them, and re-layouts  1.92 us
  transfers between devices with their start and end apart: 2, of which 0 were waited for; matrix products, arithmetic and copies ran while one was open for 3% of the time, Pallas kernels for 0%

commit v1 on v0

--- a/solution.py
+++ b/solution.py
@@ -46,7 +46,8 @@
 
 def orders(n):
     bits = bits_of(n)
-    return (bits, bits[:1] + bits[2:] + bits[1:2])
+    late = bits[:1] + bits[2:] + bits[1:2]
+    return (bits, late, bits, bits)
 
 
 def rank_of(dest, order):
@@ -60,8 +61,15 @@
     q = pl.program_id(0)
     planes, height, depth = own.shape[1:]
 
+    def add_rows(base):
+        for e in range(128):
+            at = place[elist[base + e]]
+            table = tables[e % banks]
+            table[pl.ds(at, 1), :] += rows[e:e + 1, :]
+
     @pl.when(q == 0)
     def _():
+        rows[...] = jnp.zeros_like(rows)
         ext[:, :HALO] = before[...]
         ext[:, HALO:HALO + planes] = own[...]
         ext[:, HALO + planes:] = after[...]
@@ -101,6 +109,7 @@
 
     @pl.loop(0, height // 16)
     def _(j):
+        add_rows(jnp.maximum(q * (height * SLOTS) + j * 128 - 128, 0))
         parts = []
         for g in range(2):
             z0 = pl.multiple_of(j * 16 + g * 8, 8)
@@ -132,18 +141,10 @@
             parts.append(jnp.concatenate(pieces, 0))
         block = jnp.concatenate(parts, 1)
         rows[...] = jnp.transpose(jnp.concatenate([block, jnp.zeros_like(block)], 0), (1, 0))
-        base = q * (height * SLOTS) + j * 128
-
-        @pl.loop(0, 128 // 8)
-        def _(k8):
-            for u in range(8):
-                e = k8 * 8 + u
-                at = place[elist[base + e]]
-                table = tables[u % banks]
-                table[pl.ds(at, 1), :] += rows[pl.ds(e, 1), :]
 
     @pl.when(q == pl.num_programs(0) - 1)
     def _():
+        add_rows(planes * height * SLOTS - 128)
         tile = out.shape[2]
         low_lane = lax.broadcasted_iota(jnp.int32, (tile, 128), 1) < FEAT
 
@@ -206,10 +207,10 @@
         else:
             acc[k][p] = source[pl.ds(mine * size, size)] + recv[k][p]
 
-    for p in range(2):
+    for p in range(len(lists)):
         start(p, 0)
     for k in range(count):
-        for p in range(2):
+        for p in range(len(lists)):
             finish(p, k)
             if k + 1 < count:
                 start(p, k + 1)
@@ -228,8 +229,9 @@
     n = lax.axis_size("xy")
     edges = edge_home.shape[0]
     e_dev = edges // n
-    tile = e_dev // 4
     lists = orders(n)
+    parts = len(lists)
+    tile = e_dev // (2 * parts)
     dequant = affinity.astype(jnp.float32) * block_scale[..., None]
     up = [(i, i + 1) for i in range(n - 1)]
     down = [(j, i) for i, j in up]
@@ -237,9 +239,9 @@
     after = lax.ppermute(dequant, "xy", down)
 
     dest, inner = edge_home // e_dev, edge_home % e_dev
-    half, inner = inner // (2 * tile), inner % (2 * tile)
+    half, inner = inner // (parts * tile), inner % (parts * tile)
     part, row = inner // tile, inner % tile
-    rank = jnp.where(part == 0, rank_of(dest, lists[0]), rank_of(dest, lists[1]))
+    rank = jnp.where(part == 1, rank_of(dest, lists[1]), rank_of(dest, lists[0]))
     place = ((part * n + rank) * 2 + half) * tile + row
     place = jnp.concatenate([place, jnp.full((128,), edges, jnp.int32)])
     valid = jnp.arange(SLOTS, dtype=jnp.int32) < valid_count[..., None]
@@ -259,7 +261,7 @@
     table = pl.pallas_call(
         functools.partial(sums_kernel, edges, banks),
         grid=(planes,),
-        out_shape=jax.ShapeDtypeStruct((2, n, tile, 128), jnp.float32),
+        out_shape=jax.ShapeDtypeStruct((parts, n, tile, 128), jnp.float32),
         in_specs=[whole, whole, whole, pl.BlockSpec((1, height, depth), lambda q: (q, 0, 0)), whole, whole, smem, smem],
         out_specs=whole,
         scratch_shapes=[
@@ -275,16 +277,16 @@
     sizes = [n >> (k + 1) for k in range(count)]
     total = pl.pallas_call(
         functools.partial(reduce_kernel, n, lists),
-        out_shape=jax.ShapeDtypeStruct((2, tile, 128), jnp.float32),
+        out_shape=jax.ShapeDtypeStruct((parts, tile, 128), jnp.float32),
         in_specs=[whole],
         out_specs=whole,
-        scratch_shapes=[VMEM((2, s, tile, 128), jnp.float32) for s in sizes] * 2 + [
-            pltpu.SemaphoreType.DMA((2, count)),
-            pltpu.SemaphoreType.DMA((2, count)),
+        scratch_shapes=[VMEM((parts, s, tile, 128), jnp.float32) for s in sizes] * 2 + [
+            pltpu.SemaphoreType.DMA((parts, count)),
+            pltpu.SemaphoreType.DMA((parts, count)),
         ],
         compiler_params=pltpu.CompilerParams(collective_id=0, has_side_effects=True, vmem_limit_bytes=56 << 20),
     )(table)
-    total = total.reshape(2 * tile, 128)
+    total = total.reshape(parts * tile, 128)
     return finalize(jnp.concatenate([total[:, :FEAT], total[:, FEAT:]], 0))
 
 

time: 94 us -> 84.7 us (0.901)
  Pallas kernels: 81 us -> 71.7 us
    pallas_call x1, Pallas kernels: 38.6 us -> 32.1 us  [shards(): pl.pallas_call(functools.partial(sums_kernel, edges, banks), grid=(planes...]
    pallas_call x1, Pallas kernels: 42.3 us -> 39.6 us  [shards(): pl.pallas_call(functools.partial(reduce_kernel, n, lists), out_shape=jax....]
  transfers between devices with their start and end apart: 2 -> 2, of which waited for: 0 -> 0; matrix products, arithmetic and copies ran while one was open for 3% -> 4% of each run, Pallas kernels for 0% -> 0%
where the time goes in v1:
time: 84.7 us; the launch traced here: 84.3 us
  Pallas kernels  71.7 us (85%)
  local copies, waits for them, and re-layouts  4.5 us (5%)
  starting transfers between devices  4.37 us (5%)
  other arithmetic  3.68 us (4%)
    pallas_call x1, Pallas kernels, shards(): pl.pallas_call(functools.partial(reduce_kernel, n, lists), out_shape=jax....  39.6 us
    pallas_call x1, Pallas kernels, shards(): pl.pallas_call(functools.partial(sums_kernel, edges, banks), grid=(planes...  32.1 us
    ppermute x1, starting transfers between devices, shards(): before = lax.ppermute(dequant, 'xy', up)  3.08 us
    unnamed x8, local copies, waits for them, and re-layouts  1.92 us
  transfers between devices with their start and end apart: 2, of which 0 were waited for; matrix products, arithmetic and copies ran while one was open for 4% of the time, Pallas kernels for 0%

profile of v1, /device:TPU:0, one launch (start us, length us, event | category | flops | bytes accessed | tf_op | source)
XLA Modules:
  0.0 84.3 jit_solution(2116436470136391111)
XLA Ops:
  0.0 1.3 %convert_multiply_fusion.own = f32[3,8,64,128]{3,2,1,0:T(8,128)S(1)} fusion(bf16[3,8,64,128]{3,2,1,0:T(8,128)(2,1)} %param.8, f32[3,8,64]{2,1,0:T(8,128)} %param.9), kind=kLoop, calls=%fused_computation | loop fusion | flops 393216 | bytes 1185792 | tf_op jit(solution)/shard_map/mul | solution.py:235
  1.3 0.0 copy-start
  1.3 1.3 %collective-permute-start.1 = (f32[3,8,64,128]{3,2,1,0:T(8,128)S(1)}, f32[3,8,64,128]{3,2,1,0:T(8,128)S(1)}, u32[]{:S(2)}, u32[]{:S(2)}) collective-permute-start(f32[3,8,64,128]{3,2,1,0:T(8,128)S(1)} %convert_multiply_fusion.own), channel_id=1, source_target_pairs={{1,0},{2,1},{3,2},{4,3},{5,4},{6,5},{7,6},{8,7},{9,8},{10,9},{11,1... | collective-permute-start | bytes 2359304 | tf_op jit(solution)/shard_map/ppermute | solution.py:239
  2.6 3.1 %collective-permute-start = (f32[3,8,64,128]{3,2,1,0:T(8,128)S(1)}, f32[3,8,64,128]{3,2,1,0:T(8,128)S(1)}, u32[]{:S(2)}, u32[]{:S(2)}) collective-permute-start(f32[3,8,64,128]{3,2,1,0:T(8,128)S(1)} %convert_multiply_fusion.own), channel_id=1, source_target_pairs={{0,1},{1,2},{2,3},{3,4},{4,5},{5,6},{6,7},{7,8},{8,9},{9,10},{10,1... | collective-permute-start | bytes 2359304 | tf_op jit(solution)/shard_map/ppermute | solution.py:238
  5.7 0.8 fusion.9
  6.4 0.1 copy.11
  6.6 0.8 reshape.8.elist
  7.3 1.0 %fusion.8 = s32[8192]{0:T(1024)S(1)} fusion(s32[8192]{0:T(1024)} %param.13), kind=kLoop, calls=%fused_computation.46 | loop fusion | flops 1212416 | bytes 65536 | tf_op jit(solution)/shard_map/add | solution.py:245
  8.3 0.6 concatenate.9.place
  8.9 0.0 collective-permute-done.1.after
  8.9 0.0 copy-start.1
  8.9 0.0 collective-permute-done.before
  8.9 0.0 copy-done
  8.9 0.9 %copy-done.1 = f32[3,8,64,128]{3,2,1,0:T(8,128)} copy-done((f32[3,8,64,128]{3,2,1,0:T(8,128)}, f32[3,8,64,128]{3,2,1,0:T(8,128)S(1)}, u32[]{:S(2)}) %copy-start.1) | copy-done | bytes 786456
  9.8 0.0 copy-start.2
  9.8 0.9 %copy-done.2 = f32[3,8,64,128]{3,2,1,0:T(8,128)} copy-done((f32[3,8,64,128]{3,2,1,0:T(8,128)}, f32[3,8,64,128]{3,2,1,0:T(8,128)S(1)}, u32[]{:S(2)}) %copy-start.2) | copy-done | bytes 786456
  10.7 32.1 %shard_map.82.table = f32[4,16,64,128]{3,2,1,0:T(8,128)} custom-call(f32[3,8,64,128]{3,2,1,0:T(8,128)} %copy-done.2, f32[3,8,64,128]{3,2,1,0:T(8,128)} %copy-done, f32[3,8,64,128]{3,2,1,0:T(8,128)} %copy-done.1, s32[8,64,128]{2,1,0:T(8,128)} %slots.1, bf16[4,256,256]{2,1,0:T(8,128)(2,1)} %constant.164.clone.along_y, ...), custom_call_target="tpu_custom_call" | custom-call | tf_op jit(solution)/shard_map/pallas_call | solution.py:261
  42.7 39.6 %shard_map.83 = f32[4,64,128]{2,1,0:T(8,128)} custom-call(f32[4,16,64,128]{3,2,1,0:T(8,128)} %shard_map.82.table), custom_call_target="tpu_custom_call" | custom-call | tf_op jit(solution)/shard_map/pallas_call | solution.py:278
  82.4 1.1 %fusion.18 = (f32[256,64]{1,0:T(8,128)S(1)}, f32[256,64]{1,0:T(8,128)S(1)}) fusion(f32[256,128]{1,0:T(8,128)} %bitcast.2), kind=kLoop, calls=%fused_computation.63 | loop fusion | bytes 262144 | tf_op jit(solution)/shard_map/slice | solution.py:290
  83.4 0.1 copy.14
  83.5 0.1 copy.15
  83.7 0.7 pad_maximum_fusion
  (3 shorter events, 0.0 us)
Async XLA Ops:
  1.3 7.6 %copy-start = (f32[3,8,64,128]{3,2,1,0:T(8,128)}, f32[3,8,64,128]{3,2,1,0:T(8,128)S(1)}, u32[]{:S(2)}) copy-start(f32[3,8,64,128]{3,2,1,0:T(8,128)S(1)} %convert_multiply_fusion.own) | copy-start | bytes 2359300
  1.3 7.6 %collective-permute-start.1 = (f32[3,8,64,128]{3,2,1,0:T(8,128)S(1)}, f32[3,8,64,128]{3,2,1,0:T(8,128)S(1)}, u32[]{:S(2)}, u32[]{:S(2)}) collective-permute-start(f32[3,8,64,128]{3,2,1,0:T(8,128)S(1)} %convert_multiply_fusion.own), channel_id=1, source_target_pairs={{1,0},{2,1},{3,2},{4,3},{5,4},{6,5},{7,6},{8,7},{9,8},{10,9},{11,1... | collective-permute-start | bytes 2359304 | tf_op jit(solution)/shard_map/ppermute | solution.py:239
  2.6 6.3 %collective-permute-start = (f32[3,8,64,128]{3,2,1,0:T(8,128)S(1)}, f32[3,8,64,128]{3,2,1,0:T(8,128)S(1)}, u32[]{:S(2)}, u32[]{:S(2)}) collective-permute-start(f32[3,8,64,128]{3,2,1,0:T(8,128)S(1)} %convert_multiply_fusion.own), channel_id=1, source_target_pairs={{0,1},{1,2},{2,3},{3,4},{4,5},{5,6},{6,7},{7,8},{8,9},{9,10},{10,1... | collective-permute-start | bytes 2359304 | tf_op jit(solution)/shard_map/ppermute | solution.py:238
  8.9 0.9 %copy-start.1 = (f32[3,8,64,128]{3,2,1,0:T(8,128)}, f32[3,8,64,128]{3,2,1,0:T(8,128)S(1)}, u32[]{:S(2)}) copy-start(f32[3,8,64,128]{3,2,1,0:T(8,128)S(1)} %collective-permute-done.1.after) | copy-start | bytes 2359300
  9.8 0.9 %copy-start.2 = (f32[3,8,64,128]{3,2,1,0:T(8,128)}, f32[3,8,64,128]{3,2,1,0:T(8,128)S(1)}, u32[]{:S(2)}) copy-start(f32[3,8,64,128]{3,2,1,0:T(8,128)S(1)} %collective-permute-done.before) | copy-start | bytes 2359300

commit v2 on v1

--- a/solution.py
+++ b/solution.py
@@ -57,9 +57,119 @@
     return rank
 
 
-def sums_kernel(edges, banks, before, own, after, slots, along_y, along_z, elist, place, out, ext, resp, prod, rows, *tables):
+def blur_kernel(own, along_y, along_z, out, ext, send_sem, recv_sem):
+    planes, height, depth = own.shape[1:]
+    n = lax.axis_size("xy")
+    me = lax.axis_index("xy")
+    part_id = lax.axis_index("parts")
+    has_left, has_right = me > 0, me < n - 1
+    left, right = (part_id, me - 1), (part_id, me + 1)
+    barrier = pltpu.get_barrier_semaphore()
+
+    for there, device in ((has_left, left), (has_right, right)):
+        @pl.when(there)
+        def _():
+            pl.semaphore_signal(barrier, inc=1, device_id=device, device_id_type=MESH)
+    inside = jnp.logical_and(has_left, has_right)
+
+    @pl.when(inside)
+    def _():
+        pl.semaphore_wait(barrier, 2)
+
+    @pl.when(jnp.logical_and(jnp.logical_not(inside), n > 1))
+    def _():
+        pl.semaphore_wait(barrier, 1)
+
+    def to_right(p):
+        return pltpu.make_async_remote_copy(
+            src_ref=own.at[:, p], dst_ref=ext.at[:, p],
+            send_sem=send_sem.at[0, p], recv_sem=recv_sem.at[0, p],
+            device_id=right, device_id_type=MESH)
+
+    def to_left(p):
+        return pltpu.make_async_remote_copy(
+            src_ref=own.at[:, p], dst_ref=ext.at[:, HALO + planes + p],
+            send_sem=send_sem.at[1, p], recv_sem=recv_sem.at[1, p],
+            device_id=left, device_id_type=MESH)
+
+    @pl.when(has_right)
+    def _():
+        for p in reversed(range(planes)):
+            to_right(p).start()
+
+    @pl.when(has_left)
+    def _():
+        for p in range(planes):
+            to_left(p).start()
+
+    ext[:, HALO:HALO + planes] = own[...]
+
+    @pl.when(jnp.logical_not(has_left))
+    def _():
+        ext[:, :HALO] = jnp.zeros((3, HALO, height, depth), jnp.float32)
+
+    @pl.when(jnp.logical_not(has_right))
+    def _():
+        ext[:, HALO + planes:] = jnp.zeros((3, HALO, height, depth), jnp.float32)
+
+    def need(low, high):
+        @pl.when(has_left)
+        def _():
+            to_right(low).wait_recv()
+
+        @pl.when(has_right)
+        def _():
+            to_left(high).wait_recv()
+
+    middle = planes // 2
+    for p in range(middle):
+        need(planes - 1 - p, p)
+
+    weights = [taps(s) for s in SIGMAS]
+
+    @pl.loop(0, middle)
+    def _(step):
+        need(middle - 1 - step, middle + step)
+        for q in (middle - 1 - step, middle + step):
+            crossed = [[] for _ in SIGMAS]
+            for c in range(3):
+                chunks = [[] for _ in SIGMAS]
+                for z in range(0, height, 16):
+                    mid = ext[c, q + HALO, z:z + 16, :]
+                    acc = [mid * float(w[HALO]) for w in weights]
+                    for t in range(1, HALO + 1):
+                        both = ext[c, q + HALO - t, z:z + 16, :] + ext[c, q + HALO + t, z:z + 16, :]
+                        acc = [a + both * float(w[HALO + t]) for a, w in zip(acc, weights)]
+                    for i in range(4):
+                        chunks[i].append(acc[i])
+                for i in range(4):
+                    crossed[i].append(jnp.concatenate(chunks[i], 0))
+            for i in range(4):
+                high, low = split(jnp.concatenate(crossed[i], 0))
+                wide = jnp.dot(jnp.concatenate([high, low], 1), along_y[i], preferred_element_type=jnp.float32)
+                field = wide[:, :depth] + wide[:, depth:]
+                high, low = split(field)
+                highs = jnp.concatenate([high[c * height:(c + 1) * height] for c in range(3)], 1)
+                lows = jnp.concatenate([low[c * height:(c + 1) * height] for c in range(3)], 1)
+                stacked = jnp.concatenate([highs, lows, highs, lows], 0)
+                done = jnp.dot(along_z[i], stacked, preferred_element_type=jnp.float32)
+                for c in range(3):
+                    out[q, 3 * i + c] = done[:, c * depth:(c + 1) * depth]
+
+    @pl.when(has_right)
+    def _():
+        for p in range(planes):
+            to_right(p).wait_send()
+
+    @pl.when(has_left)
+    def _():
+        for p in range(planes):
+            to_left(p).wait_send()
+
+
+def sums_kernel(planes, banks, own, resp, slots, elist, place, out, prod, rows, *tables):
     q = pl.program_id(0)
-    planes, height, depth = own.shape[1:]
+    height = own.shape[2]
 
     def add_rows(base):
         for e in range(128):
@@ -70,39 +180,10 @@
     @pl.when(q == 0)
     def _():
         rows[...] = jnp.zeros_like(rows)
-        ext[:, :HALO] = before[...]
-        ext[:, HALO:HALO + planes] = own[...]
-        ext[:, HALO + planes:] = after[...]
         for table in tables:
             @pl.loop(0, table.shape[0] // 64)
             def _(r):
                 table[pl.ds(pl.multiple_of(r * 64, 64), 64), :] = jnp.zeros((64, 128), jnp.float32)
-
-    weights = [taps(s) for s in SIGMAS]
-    crossed = [[] for _ in SIGMAS]
-    for c in range(3):
-        chunks = [[] for _ in SIGMAS]
-        for z in range(0, height, 16):
-            mid = ext[c, q + HALO, z:z + 16, :]
-            acc = [mid * float(w[HALO]) for w in weights]
-            for t in range(1, HALO + 1):
-                both = ext[c, q + HALO - t, z:z + 16, :] + ext[c, q + HALO + t, z:z + 16, :]
-                acc = [a + both * float(w[HALO + t]) for a, w in zip(acc, weights)]
-            for i in range(4):
-                chunks[i].append(acc[i])
-        for i in range(4):
-            crossed[i].append(jnp.concatenate(chunks[i], 0))
-    for i in range(4):
-        high, low = split(jnp.concatenate(crossed[i], 0))
-        wide = jnp.dot(jnp.concatenate([high, low], 1), along_y[i], preferred_element_type=jnp.float32)
-        field = wide[:, :depth] + wide[:, depth:]
-        high, low = split(field)
-        highs = jnp.concatenate([high[c * height:(c + 1) * height] for c in range(3)], 1)
-        lows = jnp.concatenate([low[c * height:(c + 1) * height] for c in range(3)], 1)
-        stacked = jnp.concatenate([highs, lows, highs, lows], 0)
-        done = jnp.dot(along_z[i], stacked, preferred_element_type=jnp.float32)
-        for c in range(3):
-            resp[3 * i + c] = done[:, c * depth:(c + 1) * depth]
 
     slot_row = lax.broadcasted_iota(jnp.int32, (SLOTS, 128), 0)
     lane_z = lax.broadcasted_iota(jnp.int32, (8, 64), 1) // SLOTS
@@ -113,8 +194,8 @@
         parts = []
         for g in range(2):
             z0 = pl.multiple_of(j * 16 + g * 8, 8)
-            r = [resp[k, pl.ds(z0, 8), :] for k in range(12)]
-            raw = [ext[c, q + HALO, pl.ds(z0, 8), :] for c in range(3)]
+            r = [resp[0, k, pl.ds(z0, 8), :] for k in range(12)]
+            raw = [own[c, 0, pl.ds(z0, 8), :] for c in range(3)]
             square = [a * a for a in r]
             cube = [a * b for a, b in zip(square, r)]
             fourth = [a * a for a in square]
@@ -233,10 +314,6 @@
     parts = len(lists)
     tile = e_dev // (2 * parts)
     dequant = affinity.astype(jnp.float32) * block_scale[..., None]
-    up = [(i, i + 1) for i in range(n - 1)]
-    down = [(j, i) for i, j in up]
-    before = lax.ppermute(dequant, "xy", up)
-    after = lax.ppermute(dequant, "xy", down)
 
     dest, inner = edge_home // e_dev, edge_home % e_dev
     half, inner = inner // (parts * tile), inner % (parts * tile)
@@ -258,20 +335,35 @@
     banks = 4 if edges * 512 * 4 <= (24 << 20) else 1
     whole = pl.BlockSpec(memory_space=VMEM)
     smem = pl.BlockSpec(memory_space=pltpu.SMEM)
-    table = pl.pallas_call(
-        functools.partial(sums_kernel, edges, banks),
-        grid=(planes,),
-        out_shape=jax.ShapeDtypeStruct((parts, n, tile, 128), jnp.float32),
-        in_specs=[whole, whole, whole, pl.BlockSpec((1, height, depth), lambda q: (q, 0, 0)), whole, whole, smem, smem],
+    resp = pl.pallas_call(
+        blur_kernel,
+        out_shape=jax.ShapeDtypeStruct((planes, 12, height, depth), jnp.float32),
+        in_specs=[whole, whole, whole],
         out_specs=whole,
         scratch_shapes=[
             VMEM((3, planes + 2 * HALO, height, depth), jnp.float32),
-            VMEM((12, height, depth), jnp.float32),
+            pltpu.SemaphoreType.DMA((2, planes)),
+            pltpu.SemaphoreType.DMA((2, planes)),
+        ],
+        compiler_params=pltpu.CompilerParams(collective_id=1, has_side_effects=True, vmem_limit_bytes=56 << 20),
+    )(dequant, along_y, along_z)
+    table = pl.pallas_call(
+        functools.partial(sums_kernel, planes, banks),
+        grid=(planes,),
+        out_shape=jax.ShapeDtypeStruct((parts, n, tile, 128), jnp.float32),
+        in_specs=[
+            pl.BlockSpec((3, 1, height, depth), lambda q: (0, q, 0, 0)),
+            pl.BlockSpec((1, 12, height, depth), lambda q: (q, 0, 0, 0)),
+            pl.BlockSpec((1, height, depth), lambda q: (q, 0, 0)),
+            smem, smem,
+        ],
+        out_specs=whole,
+        scratch_shapes=[
             VMEM((2, FEAT * 8, 64), jnp.float32),
             VMEM((128, 128), jnp.float32),
         ] + [VMEM((edges + 64, 128), jnp.float32)] * banks,
         compiler_params=pltpu.CompilerParams(vmem_limit_bytes=56 << 20),
-    )(before, dequant, after, slot_map, along_y, along_z, elist, place)
+    )(dequant, resp, slot_map, elist, place)
 
     count = n.bit_length() - 1
     sizes = [n >> (k + 1) for k in range(count)]

time: 84.7 us -> 84.1 us (level)
  Pallas kernels: 71.7 us -> 76.3 us
  starting transfers between devices: 4.37 us -> 0 us
  local copies, waits for them, and re-layouts: 4.5 us -> 2.74 us
  other arithmetic: 3.68 us -> 4.6 us
    pallas_call x1 -> x2, Pallas kernels: 32.1 us -> 38.5 us  [the longest x1 26.7 us: shards(): pl.pallas_call(functools.partial(sums_kernel, planes, banks), grid=(plane...]
    ppermute x2 -> x0, starting transfers between devices: 4.37 us -> none  [the longest x1 3.08 us: shards(): before = lax.ppermute(dequant, 'xy', up)]
    pallas_call x1, Pallas kernels: 39.6 us -> 37.8 us  [shards(): pl.pallas_call(functools.partial(reduce_kernel, n, lists), out_shape=jax....]
    unnamed x8 -> x2, local copies, waits for them, and re-layouts: 1.92 us -> 0.16 us
    mul x1, other arithmetic: 1.26 us -> 2.19 us  [shards(): dequant = affinity.astype(jnp.float32) * block_scale[..., None]]
  transfers between devices with their start and end apart: 2 -> 0, of which waited for: 0 -> 0; matrix products, arithmetic and copies ran while one was open for 4% -> 0% of each run, Pallas kernels for 0% -> 0%
where the time goes in v2:
time: 84.1 us; the launch traced here: 83.7 us
  Pallas kernels  76.3 us (91%)
  other arithmetic  4.6 us (5%)
  local copies, waits for them, and re-layouts  2.74 us (3%)
    pallas_call x1, Pallas kernels, shards(): pl.pallas_call(functools.partial(reduce_kernel, n, lists), out_shape=jax....  37.8 us
    pallas_call x1, Pallas kernels, shards(): pl.pallas_call(functools.partial(sums_kernel, planes, banks), grid=(plane...  26.7 us
    pallas_call x1, Pallas kernels, shards(): pl.pallas_call(blur_kernel, out_shape=jax.ShapeDtypeStruct((planes, 12, h...  11.8 us
    mul x1, other arithmetic, shards(): dequant = affinity.astype(jnp.float32) * block_scale[..., None]  2.19 us

profile of v2, /device:TPU:0, one launch (start us, length us, event | category | flops | bytes accessed | tf_op | source)
XLA Modules:
  0.0 83.7 jit_solution(2474972849686899662)
XLA Ops:
  0.0 0.8 fusion.9
  0.8 1.0 %fusion.8 = s32[8192]{0:T(1024)S(1)} fusion(s32[8192]{0:T(1024)} %param.13), kind=kLoop, calls=%fused_computation.46 | loop fusion | flops 1212416 | bytes 65536 | tf_op jit(solution)/shard_map/add | solution.py:322
  1.7 0.6 concatenate.9.place
  2.3 0.1 copy.11
  2.5 0.8 reshape.8.elist
  3.2 2.2 %convert_multiply_fusion.own = f32[3,8,64,128]{3,2,1,0:T(8,128)} fusion(bf16[3,8,64,128]{3,2,1,0:T(8,128)(2,1)} %param.8, f32[3,8,64]{2,1,0:T(8,128)} %param.9), kind=kLoop, calls=%fused_computation | loop fusion | flops 393216 | bytes 1185792 | tf_op jit(solution)/shard_map/mul | solution.py:316
  5.4 11.8 %shard_map.82.resp = f32[8,12,64,128]{3,2,1,0:T(8,128)} custom-call(f32[3,8,64,128]{3,2,1,0:T(8,128)} %convert_multiply_fusion.own, bf16[4,256,256]{2,1,0:T(8,128)(2,1)} %constant.164.clone.along_y, bf16[4,64,256]{2,1,0:T(8,128)(2,1)} %constant.165.clone.along_z), custom_call_target="tpu_custom_call" | custom-call | tf_op jit(solution)/shard_map/pallas_call | solution.py:338
  17.2 26.7 %shard_map.83.table = f32[4,16,64,128]{3,2,1,0:T(8,128)} custom-call(f32[3,8,64,128]{3,2,1,0:T(8,128)} %convert_multiply_fusion.own, f32[8,12,64,128]{3,2,1,0:T(8,128)} %shard_map.82.resp, s32[8,64,128]{2,1,0:T(8,128)} %slots.1, s32[4096]{0:T(1024)} %reshape.8.elist, s32[8320]{0:T(1024)} %concatenate.9.place), custom_call_target="tpu_custom_call" | custom-call | tf_op jit(solution)/shard_map/pallas_call | solution.py:350
  43.9 37.8 %shard_map.84 = f32[4,64,128]{2,1,0:T(8,128)} custom-call(f32[4,16,64,128]{3,2,1,0:T(8,128)} %shard_map.83.table), custom_call_target="tpu_custom_call" | custom-call | tf_op jit(solution)/shard_map/pallas_call | solution.py:370
  81.8 1.1 %fusion.18 = (f32[256,64]{1,0:T(8,128)S(1)}, f32[256,64]{1,0:T(8,128)S(1)}) fusion(f32[256,128]{1,0:T(8,128)} %bitcast.2), kind=kLoop, calls=%fused_computation.63 | loop fusion | bytes 262144 | tf_op jit(solution)/shard_map/slice | solution.py:382
  82.8 0.1 copy.14
  82.9 0.1 copy.15
  83.1 0.7 pad_maximum_fusion
  (3 shorter events, 0.0 us)

commit v3 on v2

--- a/solution.py
+++ b/solution.py
@@ -57,8 +57,8 @@
     return rank
 
 
-def blur_kernel(own, along_y, along_z, out, ext, send_sem, recv_sem):
-    planes, height, depth = own.shape[1:]
+def blur_kernel(lists, affinity, scale, homes, along_y, along_z, out, own, place, ext, send_sem, recv_sem):
+    planes, height, depth = affinity.shape[1:]
     n = lax.axis_size("xy")
     me = lax.axis_index("xy")
     part_id = lax.axis_index("parts")
@@ -70,6 +70,11 @@
         @pl.when(there)
         def _():
             pl.semaphore_signal(barrier, inc=1, device_id=device, device_id_type=MESH)
+    for c in range(3):
+        columns = jnp.transpose(scale[c], (1, 0))
+        for p in range(planes):
+            ext[c, HALO + p] = affinity[c, p].astype(jnp.float32) * columns[:, p:p + 1]
+
     inside = jnp.logical_and(has_left, has_right)
 
     @pl.when(inside)
@@ -82,13 +87,13 @@
 
     def to_right(p):
         return pltpu.make_async_remote_copy(
-            src_ref=own.at[:, p], dst_ref=ext.at[:, p],
+            src_ref=ext.at[:, HALO + p], dst_ref=ext.at[:, p],
             send_sem=send_sem.at[0, p], recv_sem=recv_sem.at[0, p],
             device_id=right, device_id_type=MESH)
 
     def to_left(p):
         return pltpu.make_async_remote_copy(
-            src_ref=own.at[:, p], dst_ref=ext.at[:, HALO + planes + p],
+            src_ref=ext.at[:, HALO + p], dst_ref=ext.at[:, HALO + planes + p],
             send_sem=send_sem.at[1, p], recv_sem=recv_sem.at[1, p],
             device_id=left, device_id_type=MESH)
 
@@ -102,7 +107,18 @@
         for p in range(planes):
             to_left(p).start()
 
-    ext[:, HALO:HALO + planes] = own[...]
+    own[...] = ext[:, HALO:HALO + planes]
+    rows = homes.shape[0]
+    e_dev = rows * 128 // n
+    parts = len(lists)
+    tile = e_dev // (2 * parts)
+    home = homes[...]
+    dest, inner = home // e_dev, home % e_dev
+    half, inner = inner // (parts * tile), inner % (parts * tile)
+    part, row = inner // tile, inner % tile
+    rank = jnp.where(part == 1, rank_of(dest, lists[1]), rank_of(dest, lists[0]))
+    place[:rows, :] = ((part * n + rank) * 2 + half) * tile + row
+    place[rows:, :] = jnp.full((8, 128), rows * 128, jnp.int32)
 
     @pl.when(jnp.logical_not(has_left))
     def _():
@@ -167,7 +183,7 @@
             to_left(p).wait_send()
 
 
-def sums_kernel(planes, banks, own, resp, slots, elist, place, out, prod, rows, *tables):
+def sums_kernel(planes, banks, own, resp, slots, elist, place, out, rows, *tables):
     q = pl.program_id(0)
     height = own.shape[2]
 
@@ -186,12 +202,20 @@
                 table[pl.ds(pl.multiple_of(r * 64, 64), 64), :] = jnp.zeros((64, 128), jnp.float32)
 
     slot_row = lax.broadcasted_iota(jnp.int32, (SLOTS, 128), 0)
-    lane_z = lax.broadcasted_iota(jnp.int32, (8, 64), 1) // SLOTS
+    lane = lax.broadcasted_iota(jnp.int32, (8, 128), 1)
+    lane_z = (lane // SLOTS) % 8
+    spread = (lax.broadcasted_iota(jnp.int32, (8, 128), 0) + 8 - lane_z) % 8
 
     @pl.loop(0, height // 16)
     def _(j):
         add_rows(jnp.maximum(q * (height * SLOTS) + j * 128 - 128, 0))
-        parts = []
+        z16 = pl.multiple_of(j * 16, 16)
+        slot = slots[0, pl.ds(z16, 16), :]
+        hot = jnp.concatenate([
+            (jnp.broadcast_to(slot[k:k + 1, :], (SLOTS, 128)) == slot_row).astype(jnp.float32) for k in range(16)
+        ], 0).astype(jnp.bfloat16)
+        rhs = jnp.concatenate([hot, hot], 1)
+        groups = []
         for g in range(2):
             z0 = pl.multiple_of(j * 16 + g * 8, 8)
             r = [resp[0, k, pl.ds(z0, 8), :] for k in range(12)]
@@ -204,23 +228,21 @@
                 a, b, c = r[3 * i:3 * i + 3]
                 pairs += [a * b, a * c, b * c]
             ones = [jnp.ones((8, 128), jnp.float32)]
-            feats = jnp.concatenate(r + square + cube + fourth + pairs + raw + ones, 0)
+            groups.append(r + square + cube + fourth + pairs + raw + ones)
+        pieces = []
+        for f in range(0, FEAT, 8):
+            feats = jnp.concatenate(groups[0][f:f + 8] + groups[1][f:f + 8], 0)
             high, low = split(feats)
             lhs = jnp.concatenate([high, low], 1)
-            slot = slots[0, pl.ds(z0, 8), :]
-            hot = jnp.concatenate([
-                (jnp.broadcast_to(slot[k:k + 1, :], (SLOTS, 128)) == slot_row).astype(jnp.float32) for k in range(8)
-            ], 0).astype(jnp.bfloat16)
-            rhs = jnp.concatenate([hot, hot], 1)
-            prod[g] = lax.dot_general(lhs, rhs, (((1,), (1,)), ((), ())), preferred_element_type=jnp.float32)
-            pieces = []
-            for f in range(0, FEAT, 8):
-                piece = prod[g, pl.ds(f * 8, 8, stride=8), :]
-                for k in range(1, 8):
-                    piece = jnp.where(lane_z == k, prod[g, pl.ds(f * 8 + k, 8, stride=8), :], piece)
-                pieces.append(piece)
-            parts.append(jnp.concatenate(pieces, 0))
-        block = jnp.concatenate(parts, 1)
+            prod = lax.dot_general(lhs, rhs, (((1,), (1,)), ((), ())), preferred_element_type=jnp.float32)
+            piece = None
+            for k in range(8):
+                both = jnp.where(lane < 64, prod[k * 8:k * 8 + 8], prod[64 + k * 8:64 + k * 8 + 8])
+                piece = both if k == 0 else jnp.where(spread == k, pltpu.roll(both, k, 0), piece)
+            for bit in (1, 2, 4):
+                piece = jnp.where((lane_z // bit) % 2 == 1, pltpu.roll(piece, 8 - bit, 0), piece)
+            pieces.append(piece)
+        block = jnp.concatenate(pieces, 0)
         rows[...] = jnp.transpose(jnp.concatenate([block, jnp.zeros_like(block)], 0), (1, 0))
 
     @pl.when(q == pl.num_programs(0) - 1)
@@ -313,14 +335,6 @@
     lists = orders(n)
     parts = len(lists)
     tile = e_dev // (2 * parts)
-    dequant = affinity.astype(jnp.float32) * block_scale[..., None]
-
-    dest, inner = edge_home // e_dev, edge_home % e_dev
-    half, inner = inner // (parts * tile), inner % (parts * tile)
-    part, row = inner // tile, inner % tile
-    rank = jnp.where(part == 1, rank_of(dest, lists[1]), rank_of(dest, lists[0]))
-    place = ((part * n + rank) * 2 + half) * tile + row
-    place = jnp.concatenate([place, jnp.full((128,), edges, jnp.int32)])
     valid = jnp.arange(SLOTS, dtype=jnp.int32) < valid_count[..., None]
     elist = jnp.where(valid, edge_list, edges).reshape(-1)
 
@@ -335,18 +349,22 @@
     banks = 4 if edges * 512 * 4 <= (24 << 20) else 1
     whole = pl.BlockSpec(memory_space=VMEM)
     smem = pl.BlockSpec(memory_space=pltpu.SMEM)
-    resp = pl.pallas_call(
-        blur_kernel,
-        out_shape=jax.ShapeDtypeStruct((planes, 12, height, depth), jnp.float32),
-        in_specs=[whole, whole, whole],
-        out_specs=whole,
+    resp, dequant, place = pl.pallas_call(
+        functools.partial(blur_kernel, lists),
+        out_shape=[
+            jax.ShapeDtypeStruct((planes, 12, height, depth), jnp.float32),
+            jax.ShapeDtypeStruct((3, planes, height, depth), jnp.float32),
+            jax.ShapeDtypeStruct((edges // 128 + 8, 128), jnp.int32),
+        ],
+        in_specs=[whole] * 5,
+        out_specs=[whole] * 3,
         scratch_shapes=[
             VMEM((3, planes + 2 * HALO, height, depth), jnp.float32),
             pltpu.SemaphoreType.DMA((2, planes)),
             pltpu.SemaphoreType.DMA((2, planes)),
         ],
         compiler_params=pltpu.CompilerParams(collective_id=1, has_side_effects=True, vmem_limit_bytes=56 << 20),
-    )(dequant, along_y, along_z)
+    )(affinity, block_scale, edge_home.reshape(edges // 128, 128), along_y, along_z)
     table = pl.pallas_call(
         functools.partial(sums_kernel, planes, banks),
         grid=(planes,),
@@ -359,11 +377,10 @@
         ],
         out_specs=whole,
         scratch_shapes=[
-            VMEM((2, FEAT * 8, 64), jnp.float32),
             VMEM((128, 128), jnp.float32),
         ] + [VMEM((edges + 64, 128), jnp.float32)] * banks,
         compiler_params=pltpu.CompilerParams(vmem_limit_bytes=56 << 20),
-    )(dequant, resp, slot_map, elist, place)
+    )(dequant, resp, slot_map, elist, place.reshape(-1))
 
     count = n.bit_length() - 1
     sizes = [n >> (k + 1) for k in range(count)]

time: 84.1 us -> 78.5 us (0.933)
  other arithmetic: 4.6 us -> 1.46 us
  Pallas kernels: 76.3 us -> 74.5 us
    mul x1 -> x0, other arithmetic: 2.19 us -> none  [shards(): dequant = affinity.astype(jnp.float32) * block_scale[..., None]]
    pallas_call x1, Pallas kernels: 26.7 us -> 24.6 us  [shards(): pl.pallas_call(functools.partial(sums_kernel, planes, banks), grid=(plane...]
    add x1 -> x0, other arithmetic: 0.96 us -> none  [shards(): place = ((part * n + rank) * 2 + half) * tile + row]
where the time goes in v3:
time: 78.5 us; the launch traced here: 78.2 us
  Pallas kernels  74.5 us (95%)
  local copies, waits for them, and re-layouts  2.12 us (3%)
  other arithmetic  1.46 us (2%)
    pallas_call x1, Pallas kernels, shards(): pl.pallas_call(functools.partial(reduce_kernel, n, lists), out_shape=jax....  37.9 us
    pallas_call x1, Pallas kernels, shards(): pl.pallas_call(functools.partial(sums_kernel, planes, banks), grid=(plane...  24.6 us
    pallas_call x1, Pallas kernels, shards(): pl.pallas_call(functools.partial(blur_kernel, lists), out_shape=[jax.Shap...  11.9 us

profile of v3, /device:TPU:0, one launch (start us, length us, event | category | flops | bytes accessed | tf_op | source)
XLA Modules:
  0.0 78.2 jit_solution(5719778796921680866)
XLA Ops:
  0.0 0.8 fusion
  0.8 0.1 copy.11
  0.9 0.8 reshape.14.elist
  1.7 11.9 %shard_map.82 = (f32[8,12,64,128]{3,2,1,0:T(8,128)}, f32[3,8,64,128]{3,2,1,0:T(8,128)}, s32[72,128]{1,0:T(8,128)}) custom-call(bf16[3,8,64,128]{3,2,1,0:T(8,128)(2,1)} %affinity.1, f32[3,8,64]{2,1,0:T(8,128)} %scale.1, s32[64,128]{1,0:T(8,128)} %bitcast.6, bf16[4,256,256]{2,1,0:T(8,128)(2,1)} %constant.8.clone.along_y, bf16[4,64,256]{2,1,0:T(8,128)(2,1)} %constant.9.clone.along_z), custom_call_target="tpu_custom_call" | custom-call | tf_op jit(solution)/shard_map/pallas_call | solution.py:352
  13.6 24.6 %shard_map.83.table = f32[4,16,64,128]{3,2,1,0:T(8,128)} custom-call(f32[3,8,64,128]{3,2,1,0:T(8,128)} %get-tuple-element.8.own, f32[8,12,64,128]{3,2,1,0:T(8,128)} %get-tuple-element.9.resp, s32[8,64,128]{2,1,0:T(8,128)} %slots.1, s32[4096]{0:T(1024)} %reshape.14.elist, s32[9216]{0:T(1024)} %bitcast.5), custom_call_target="tpu_custom_call" | custom-call | tf_op jit(solution)/shard_map/pallas_call | solution.py:368
  38.3 37.9 %shard_map.84 = f32[4,64,128]{2,1,0:T(8,128)} custom-call(f32[4,16,64,128]{3,2,1,0:T(8,128)} %shard_map.83.table), custom_call_target="tpu_custom_call" | custom-call | tf_op jit(solution)/shard_map/pallas_call | solution.py:387
  76.2 1.1 %fusion.1 = (f32[256,64]{1,0:T(8,128)S(1)}, f32[256,64]{1,0:T(8,128)S(1)}) fusion(f32[256,128]{1,0:T(8,128)} %bitcast.4), kind=kLoop, calls=%fused_computation.6 | loop fusion | bytes 262144 | tf_op jit(solution)/shard_map/slice | solution.py:399
  77.3 0.1 copy.14
  77.4 0.1 copy.15
  77.5 0.7 pad_maximum_fusion
  (3 shorter events, 0.0 us)

commit v4 on v3

--- a/solution.py
+++ b/solution.py
@@ -128,49 +128,56 @@
     def _():
         ext[:, HALO + planes:] = jnp.zeros((3, HALO, height, depth), jnp.float32)
 
-    def need(low, high):
-        @pl.when(has_left)
+    side = me % 2
+    even, odd = side == 0, side == 1
+
+    @pl.when(jnp.logical_and(even, has_right))
+    def _():
+        for p in range(planes):
+            to_left(p).wait_recv()
+
+    @pl.when(jnp.logical_and(odd, has_left))
+    def _():
+        for p in range(planes):
+            to_right(p).wait_recv()
+
+    weights = [taps(s) for s in SIGMAS]
+
+    @pl.loop(0, planes)
+    def _(step):
+        @pl.when(jnp.logical_and(even, has_left))
         def _():
-            to_right(low).wait_recv()
-
-        @pl.when(has_right)
+            to_right(planes - 1 - step).wait_recv()
+
+        @pl.when(jnp.logical_and(odd, has_right))
         def _():
-            to_left(high).wait_recv()
-
-    middle = planes // 2
-    for p in range(middle):
-        need(planes - 1 - p, p)
-
-    weights = [taps(s) for s in SIGMAS]
-
-    @pl.loop(0, middle)
-    def _(step):
-        need(middle - 1 - step, middle + step)
-        for q in (middle - 1 - step, middle + step):
-            crossed = [[] for _ in SIGMAS]
+            to_left(step).wait_recv()
+
+        q = step + (1 - side) * (planes - 1 - 2 * step)
+        crossed = [[] for _ in SIGMAS]
+        for c in range(3):
+            chunks = [[] for _ in SIGMAS]
+            for z in range(0, height, 16):
+                mid = ext[c, q + HALO, z:z + 16, :]
+                acc = [mid * float(w[HALO]) for w in weights]
+                for t in range(1, HALO + 1):
+                    both = ext[c, q + HALO - t, z:z + 16, :] + ext[c, q + HALO + t, z:z + 16, :]
+                    acc = [a + both * float(w[HALO + t]) for a, w in zip(acc, weights)]
+                for i in range(4):
+                    chunks[i].append(acc[i])
+            for i in range(4):
+                crossed[i].append(jnp.concatenate(chunks[i], 0))
+        for i in range(4):
+            high, low = split(jnp.concatenate(crossed[i], 0))
+            wide = jnp.dot(jnp.concatenate([high, low], 1), along_y[i], preferred_element_type=jnp.float32)
+            field = wide[:, :depth] + wide[:, depth:]
+            high, low = split(field)
+            highs = jnp.concatenate([high[c * height:(c + 1) * height] for c in range(3)], 1)
+            lows = jnp.concatenate([low[c * height:(c + 1) * height] for c in range(3)], 1)
+            stacked = jnp.concatenate([highs, lows, highs, lows], 0)
+            done = jnp.dot(along_z[i], stacked, preferred_element_type=jnp.float32)
             for c in range(3):
-                chunks = [[] for _ in SIGMAS]
-                for z in range(0, height, 16):
-                    mid = ext[c, q + HALO, z:z + 16, :]
-                    acc = [mid * float(w[HALO]) for w in weights]
-                    for t in range(1, HALO + 1):
-                        both = ext[c, q + HALO - t, z:z + 16, :] + ext[c, q + HALO + t, z:z + 16, :]
-                        acc = [a + both * float(w[HALO + t]) for a, w in zip(acc, weights)]
-                    for i in range(4):
-                        chunks[i].append(acc[i])
-                for i in range(4):
-                    crossed[i].append(jnp.concatenate(chunks[i], 0))
-            for i in range(4):
-                high, low = split(jnp.concatenate(crossed[i], 0))
-                wide = jnp.dot(jnp.concatenate([high, low], 1), along_y[i], preferred_element_type=jnp.float32)
-                field = wide[:, :depth] + wide[:, depth:]
-                high, low = split(field)
-                highs = jnp.concatenate([high[c * height:(c + 1) * height] for c in range(3)], 1)
-                lows = jnp.concatenate([low[c * height:(c + 1) * height] for c in range(3)], 1)
-                stacked = jnp.concatenate([highs, lows, highs, lows], 0)
-                done = jnp.dot(along_z[i], stacked, preferred_element_type=jnp.float32)
-                for c in range(3):
-                    out[q, 3 * i + c] = done[:, c * depth:(c + 1) * depth]
+                out[q, 3 * i + c] = done[:, c * depth:(c + 1) * depth]
 
     @pl.when(has_right)
     def _():
@@ -188,10 +195,16 @@
     height = own.shape[2]
 
     def add_rows(base):
-        for e in range(128):
-            at = place[elist[base + e]]
-            table = tables[e % banks]
-            table[pl.ds(at, 1), :] += rows[e:e + 1, :]
+        for e in range(0, 128, 2 * banks):
+            ats = [place[elist[base + e + u]] for u in range(2 * banks)]
+            own_rows = [rows[e + u:e + u + 1, :] for u in range(2 * banks)]
+            held = [tables[u % banks][pl.ds(ats[u], 1), :] for u in range(2 * banks)]
+            for u in range(banks):
+                again = (ats[u] == ats[u + banks]).astype(jnp.float32)
+                first = held[u] + own_rows[u]
+                second = held[u + banks] + own_rows[u + banks] + own_rows[u] * again
+                tables[u][pl.ds(ats[u], 1), :] = first
+                tables[u][pl.ds(ats[u + banks], 1), :] = second
 
     @pl.when(q == 0)
     def _():
@@ -213,8 +226,9 @@
         slot = slots[0, pl.ds(z16, 16), :]
         hot = jnp.concatenate([
             (jnp.broadcast_to(slot[k:k + 1, :], (SLOTS, 128)) == slot_row).astype(jnp.float32) for k in range(16)
-        ], 0).astype(jnp.bfloat16)
-        rhs = jnp.concatenate([hot, hot], 1)
+        ], 0)
+        hot = jnp.transpose(hot, (1, 0)).astype(jnp.bfloat16)
+        rhs = jnp.concatenate([hot, hot], 0)
         groups = []
         for g in range(2):
             z0 = pl.multiple_of(j * 16 + g * 8, 8)
@@ -234,7 +248,7 @@
             feats = jnp.concatenate(groups[0][f:f + 8] + groups[1][f:f + 8], 0)
             high, low = split(feats)
             lhs = jnp.concatenate([high, low], 1)
-            prod = lax.dot_general(lhs, rhs, (((1,), (1,)), ((), ())), preferred_element_type=jnp.float32)
+            prod = jnp.dot(lhs, rhs, preferred_element_type=jnp.float32)
             piece = None
             for k in range(8):
                 both = jnp.where(lane < 64, prod[k * 8:k * 8 + 8], prod[64 + k * 8:64 + k * 8 + 8])

time: 78.5 us -> 81.6 us (1.039)
  Pallas kernels: 74.5 us -> 77.7 us
    pallas_call x1, Pallas kernels: 24.6 us -> 28.2 us  [shards(): pl.pallas_call(functools.partial(sums_kernel, planes, banks), grid=(plane...]
    pallas_call x1, Pallas kernels: 37.9 us -> 36.2 us  [shards(): pl.pallas_call(functools.partial(reduce_kernel, n, lists), out_shape=jax....]
    pallas_call x1, Pallas kernels: 11.9 us -> 13.3 us  [shards(): pl.pallas_call(functools.partial(blur_kernel, lists), out_shape=[jax.Shap...]
where the time goes in v4:
time: 81.6 us; the launch traced here: 81.3 us
  Pallas kernels  77.7 us (95%)
  local copies, waits for them, and re-layouts  2.12 us (3%)
  other arithmetic  1.46 us (2%)
    pallas_call x1, Pallas kernels, shards(): pl.pallas_call(functools.partial(reduce_kernel, n, lists), out_shape=jax....  36.2 us
    pallas_call x1, Pallas kernels, shards(): pl.pallas_call(functools.partial(sums_kernel, planes, banks), grid=(plane...  28.2 us
    pallas_call x1, Pallas kernels, shards(): pl.pallas_call(functools.partial(blur_kernel, lists), out_shape=[jax.Shap...  13.3 us

profile of v4, /device:TPU:0, one launch (start us, length us, event | category | flops | bytes accessed | tf_op | source)
XLA Modules:
  0.0 81.3 jit_solution(16317306928237126364)
XLA Ops:
  0.0 0.8 fusion
  0.8 0.1 copy.11
  0.9 0.8 reshape.14.elist
  1.7 13.3 %shard_map.82 = (f32[8,12,64,128]{3,2,1,0:T(8,128)}, f32[3,8,64,128]{3,2,1,0:T(8,128)}, s32[72,128]{1,0:T(8,128)}) custom-call(bf16[3,8,64,128]{3,2,1,0:T(8,128)(2,1)} %affinity.1, f32[3,8,64]{2,1,0:T(8,128)} %scale.1, s32[64,128]{1,0:T(8,128)} %bitcast.6, bf16[4,256,256]{2,1,0:T(8,128)(2,1)} %constant.8.clone.along_y, bf16[4,64,256]{2,1,0:T(8,128)(2,1)} %constant.9.clone.along_z), custom_call_target="tpu_custom_call" | custom-call | tf_op jit(solution)/shard_map/pallas_call | solution.py:366
  15.0 28.2 %shard_map.83.table = f32[4,16,64,128]{3,2,1,0:T(8,128)} custom-call(f32[3,8,64,128]{3,2,1,0:T(8,128)} %get-tuple-element.8.own, f32[8,12,64,128]{3,2,1,0:T(8,128)} %get-tuple-element.9.resp, s32[8,64,128]{2,1,0:T(8,128)} %slots.1, s32[4096]{0:T(1024)} %reshape.14.elist, s32[9216]{0:T(1024)} %bitcast.5), custom_call_target="tpu_custom_call" | custom-call | tf_op jit(solution)/shard_map/pallas_call | solution.py:382
  43.1 36.2 %shard_map.84 = f32[4,64,128]{2,1,0:T(8,128)} custom-call(f32[4,16,64,128]{3,2,1,0:T(8,128)} %shard_map.83.table), custom_call_target="tpu_custom_call" | custom-call | tf_op jit(solution)/shard_map/pallas_call | solution.py:401
  79.3 1.1 %fusion.1 = (f32[256,64]{1,0:T(8,128)S(1)}, f32[256,64]{1,0:T(8,128)S(1)}) fusion(f32[256,128]{1,0:T(8,128)} %bitcast.4), kind=kLoop, calls=%fused_computation.6 | loop fusion | bytes 262144 | tf_op jit(solution)/shard_map/slice | solution.py:413
  80.4 0.1 copy.14
  80.5 0.1 copy.15
  80.6 0.7 pad_maximum_fusion
  (3 shorter events, 0.0 us)

commit v5 on v4

--- a/solution.py
+++ b/solution.py
@@ -195,16 +195,10 @@
     height = own.shape[2]
 
     def add_rows(base):
-        for e in range(0, 128, 2 * banks):
-            ats = [place[elist[base + e + u]] for u in range(2 * banks)]
-            own_rows = [rows[e + u:e + u + 1, :] for u in range(2 * banks)]
-            held = [tables[u % banks][pl.ds(ats[u], 1), :] for u in range(2 * banks)]
-            for u in range(banks):
-                again = (ats[u] == ats[u + banks]).astype(jnp.float32)
-                first = held[u] + own_rows[u]
-                second = held[u + banks] + own_rows[u + banks] + own_rows[u] * again
-                tables[u][pl.ds(ats[u], 1), :] = first
-                tables[u][pl.ds(ats[u + banks], 1), :] = second
+        for e in range(128):
+            at = place[elist[base + e]]
+            table = tables[e % banks]
+            table[pl.ds(at, 1), :] += rows[e:e + 1, :]
 
     @pl.when(q == 0)
     def _():
@@ -226,9 +220,8 @@
         slot = slots[0, pl.ds(z16, 16), :]
         hot = jnp.concatenate([
             (jnp.broadcast_to(slot[k:k + 1, :], (SLOTS, 128)) == slot_row).astype(jnp.float32) for k in range(16)
-        ], 0)
-        hot = jnp.transpose(hot, (1, 0)).astype(jnp.bfloat16)
-        rhs = jnp.concatenate([hot, hot], 0)
+        ], 0).astype(jnp.bfloat16)
+        rhs = jnp.concatenate([hot, hot], 1)
         groups = []
         for g in range(2):
             z0 = pl.multiple_of(j * 16 + g * 8, 8)
@@ -248,7 +241,7 @@
             feats = jnp.concatenate(groups[0][f:f + 8] + groups[1][f:f + 8], 0)
             high, low = split(feats)
             lhs = jnp.concatenate([high, low], 1)
-            prod = jnp.dot(lhs, rhs, preferred_element_type=jnp.float32)
+            prod = lax.dot_general(lhs, rhs, (((1,), (1,)), ((), ())), preferred_element_type=jnp.float32)
             piece = None
             for k in range(8):
                 both = jnp.where(lane < 64, prod[k * 8:k * 8 + 8], prod[64 + k * 8:64 + k * 8 + 8])
@@ -296,6 +289,7 @@
     pl.semaphore_wait(barrier, count)
 
     copies = {}
+    lane = lax.broadcasted_iota(jnp.int32, table.shape[2:], 1)
 
     def start(p, k):
         bit = lists[p][k]
@@ -320,7 +314,14 @@
         source = table.at[p] if k == 0 else acc[k - 1].at[p]
         copies[p, k].wait_recv()
         if k == count - 1:
-            out[p] = source[mine] + recv[k][p, 0]
+            total = source[mine] + recv[k][p, 0]
+            tile = total.shape[0]
+            last = (lane % FEAT) == FEAT - 1
+            low = jnp.where(lane < FEAT, total[:, FEAT - 1:FEAT], total[:, 2 * FEAT - 1:])
+            done = jnp.where(last, jnp.log1p(total), total / jnp.maximum(low, 1.0))
+            out[p * tile:(p + 1) * tile, :] = done[:, :FEAT]
+            base = (len(lists) + p) * tile
+            out[base:base + tile, :] = done[:, FEAT:]
         else:
             acc[k][p] = source[pl.ds(mine * size, size)] + recv[k][p]
 
@@ -333,12 +334,6 @@
                 start(p, k + 1)
     for copy in copies.values():
         copy.wait_send()
-
-
-def finalize(table):
-    count = table[:, FEAT - 1:]
-    means = table[:, :FEAT - 1] / jnp.maximum(count, 1.0)
-    return jnp.concatenate([means, jnp.log1p(count)], 1)
 
 
 def shards(affinity, block_scale, slot_map, edge_list, valid_count, edge_home):
@@ -360,7 +355,7 @@
         zs.append(np.concatenate([high, high, low, low], 1))
     along_y = jnp.asarray(np.stack(ys), jnp.bfloat16)
     along_z = jnp.asarray(np.stack(zs), jnp.bfloat16)
-    banks = 4 if edges * 512 * 4 <= (24 << 20) else 1
+    banks = 2 if edges * 512 * 4 <= (24 << 20) else 1
     whole = pl.BlockSpec(memory_space=VMEM)
     smem = pl.BlockSpec(memory_space=pltpu.SMEM)
     resp, dequant, place = pl.pallas_call(
@@ -398,9 +393,9 @@
 
     count = n.bit_length() - 1
     sizes = [n >> (k + 1) for k in range(count)]
-    total = pl.pallas_call(
+    return pl.pallas_call(
         functools.partial(reduce_kernel, n, lists),
-        out_shape=jax.ShapeDtypeStruct((parts, tile, 128), jnp.float32),
+        out_shape=jax.ShapeDtypeStruct((e_dev, FEAT), jnp.float32),
         in_specs=[whole],
         out_specs=whole,
         scratch_shapes=[VMEM((parts, s, tile, 128), jnp.float32) for s in sizes] * 2 + [
@@ -409,8 +404,6 @@
         ],
         compiler_params=pltpu.CompilerParams(collective_id=0, has_side_effects=True, vmem_limit_bytes=56 << 20),
     )(table)
-    total = total.reshape(parts * tile, 128)
-    return finalize(jnp.concatenate([total[:, :FEAT], total[:, FEAT:]], 0))
 
 
 def solution(mesh):

time: 81.6 us -> 77.9 us (0.955)
  Pallas kernels: 77.7 us -> 73.8 us
    pallas_call x1, Pallas kernels: 28.2 us -> 24.3 us  [shards(): pl.pallas_call(functools.partial(sums_kernel, planes, banks), grid=(plane...]
    pallas_call x0 -> x1, local copies, waits for them, and re-layouts: none -> 1.72 us  [shards(): pl.pallas_call(functools.partial(reduce_kernel, n, lists), out_shape=jax....]
    slice x1 -> x0, local copies, waits for them, and re-layouts: 1.07 us -> none  [shards(): return finalize(jnp.concatenate([total[:, :FEAT], total[:, FEAT:]], 0))]
where the time goes in v5:
time: 77.9 us; the launch traced here: 77.2 us
  Pallas kernels  73.8 us (95%)
  local copies, waits for them, and re-layouts  2.6 us (3%)
    pallas_call x1, Pallas kernels, shards(): pl.pallas_call(functools.partial(reduce_kernel, n, lists), out_shape=jax....  36.2 us
    pallas_call x1, Pallas kernels, shards(): pl.pallas_call(functools.partial(sums_kernel, planes, banks), grid=(plane...  24.3 us
    pallas_call x1, Pallas kernels, shards(): pl.pallas_call(functools.partial(blur_kernel, lists), out_shape=[jax.Shap...  13.3 us
    pallas_call x1, local copies, waits for them, and re-layouts, shards(): pl.pallas_call(functools.partial(reduce_kernel, n, lists), out_shape=jax....  1.72 us

profile of v5, /device:TPU:0, one launch (start us, length us, event | category | flops | bytes accessed | tf_op | source)
XLA Modules:
  0.0 77.2 jit_solution(5010552730274743121)
XLA Ops:
  0.0 0.8 fusion
  0.8 0.1 copy.10
  0.9 0.8 reshape.11.elist
  1.7 13.3 %shard_map.82 = (f32[8,12,64,128]{3,2,1,0:T(8,128)}, f32[3,8,64,128]{3,2,1,0:T(8,128)}, s32[72,128]{1,0:T(8,128)}) custom-call(bf16[3,8,64,128]{3,2,1,0:T(8,128)(2,1)} %affinity.1, f32[3,8,64]{2,1,0:T(8,128)} %scale.1, s32[64,128]{1,0:T(8,128)} %bitcast.3, bf16[4,256,256]{2,1,0:T(8,128)(2,1)} %constant.6.clone.along_y, bf16[4,64,256]{2,1,0:T(8,128)(2,1)} %constant.7.clone.along_z), custom_call_target="tpu_custom_call" | custom-call | tf_op jit(solution)/shard_map/pallas_call | solution.py:361
  15.0 24.3 %shard_map.83.table = f32[4,16,64,128]{3,2,1,0:T(8,128)} custom-call(f32[3,8,64,128]{3,2,1,0:T(8,128)} %get-tuple-element.8.own, f32[8,12,64,128]{3,2,1,0:T(8,128)} %get-tuple-element.9.resp, s32[8,64,128]{2,1,0:T(8,128)} %slots.1, s32[4096]{0:T(1024)} %reshape.11.elist, s32[9216]{0:T(1024)} %bitcast.2), custom_call_target="tpu_custom_call" | custom-call | tf_op jit(solution)/shard_map/pallas_call | solution.py:377
  39.3 36.2 %shard_map.84 = f32[512,64]{1,0:T(8,128)} custom-call(f32[4,16,64,128]{3,2,1,0:T(8,128)} %shard_map.83.table), custom_call_target="tpu_custom_call" | custom-call | tf_op jit(solution)/shard_map/pallas_call | solution.py:396
  75.4 1.7 %copy.11 = f32[512,64]{0,1:T(8,128)} copy(f32[512,64]{1,0:T(8,128)} %shard_map.84) | data formatting | bytes 262144 | tf_op jit(solution)/shard_map/pallas_call | solution.py:396

commit v6 on v5

--- a/solution.py
+++ b/solution.py
@@ -57,7 +57,7 @@
     return rank
 
 
-def blur_kernel(lists, affinity, scale, homes, along_y, along_z, out, own, place, ext, send_sem, recv_sem):
+def blur_kernel(lists, affinity, scale, homes, along_y, along_z, out, own, place, ext, done_planes, send_sem, recv_sem, out_sem):
     planes, height, depth = affinity.shape[1:]
     n = lax.axis_size("xy")
     me = lax.axis_index("xy")
@@ -97,15 +97,33 @@
             send_sem=send_sem.at[1, p], recv_sem=recv_sem.at[1, p],
             device_id=left, device_id_type=MESH)
 
-    @pl.when(has_right)
-    def _():
-        for p in reversed(range(planes)):
-            to_right(p).start()
-
-    @pl.when(has_left)
-    def _():
-        for p in range(planes):
-            to_left(p).start()
+    side = me % 2
+    even, odd = side == 0, side == 1
+
+    def send_right(parity):
+        @pl.when(jnp.logical_and(parity, has_right))
+        def _():
+            for p in reversed(range(planes)):
+                to_right(p).start()
+
+    def send_left(parity):
+        @pl.when(jnp.logical_and(parity, has_left))
+        def _():
+            for p in range(planes):
+                to_left(p).start()
+
+    send_left(even)
+    send_right(odd)
+    send_right(even)
+    send_left(odd)
+
+    @pl.when(jnp.logical_not(has_left))
+    def _():
+        ext[:, :HALO] = jnp.zeros((3, HALO, height, depth), jnp.float32)
+
+    @pl.when(jnp.logical_not(has_right))
+    def _():
+        ext[:, HALO + planes:] = jnp.zeros((3, HALO, height, depth), jnp.float32)
 
     own[...] = ext[:, HALO:HALO + planes]
     rows = homes.shape[0]
@@ -119,17 +137,6 @@
     rank = jnp.where(part == 1, rank_of(dest, lists[1]), rank_of(dest, lists[0]))
     place[:rows, :] = ((part * n + rank) * 2 + half) * tile + row
     place[rows:, :] = jnp.full((8, 128), rows * 128, jnp.int32)
-
-    @pl.when(jnp.logical_not(has_left))
-    def _():
-        ext[:, :HALO] = jnp.zeros((3, HALO, height, depth), jnp.float32)
-
-    @pl.when(jnp.logical_not(has_right))
-    def _():
-        ext[:, HALO + planes:] = jnp.zeros((3, HALO, height, depth), jnp.float32)
-
-    side = me % 2
-    even, odd = side == 0, side == 1
 
     @pl.when(jnp.logical_and(even, has_right))
     def _():
@@ -177,7 +184,11 @@
             stacked = jnp.concatenate([highs, lows, highs, lows], 0)
             done = jnp.dot(along_z[i], stacked, preferred_element_type=jnp.float32)
             for c in range(3):
-                out[q, 3 * i + c] = done[:, c * depth:(c + 1) * depth]
+                done_planes[q, 3 * i + c] = done[:, c * depth:(c + 1) * depth]
+        pltpu.make_async_copy(done_planes.at[q], out.at[q], out_sem.at[q]).start()
+
+    for q in range(planes):
+        pltpu.make_async_copy(done_planes.at[q], out.at[q], out_sem.at[q]).wait()
 
     @pl.when(has_right)
     def _():
@@ -366,11 +377,13 @@
             jax.ShapeDtypeStruct((edges // 128 + 8, 128), jnp.int32),
         ],
         in_specs=[whole] * 5,
-        out_specs=[whole] * 3,
+        out_specs=[pl.BlockSpec(memory_space=pl.ANY), whole, whole],
         scratch_shapes=[
             VMEM((3, planes + 2 * HALO, height, depth), jnp.float32),
+            VMEM((planes, 12, height, depth), jnp.float32),
             pltpu.SemaphoreType.DMA((2, planes)),
             pltpu.SemaphoreType.DMA((2, planes)),
+            pltpu.SemaphoreType.DMA((planes,)),
         ],
         compiler_params=pltpu.CompilerParams(collective_id=1, has_side_effects=True, vmem_limit_bytes=56 << 20),
     )(affinity, block_scale, edge_home.reshape(edges // 128, 128), along_y, along_z)

time: 77.9 us -> 77.5 us (level)
  no operation moved by 1% of the time
where the time goes in v6:
time: 77.5 us; the launch traced here: 77.1 us
  Pallas kernels  73.8 us (95%)
  local copies, waits for them, and re-layouts  2.6 us (3%)
    pallas_call x1, Pallas kernels, shards(): pl.pallas_call(functools.partial(reduce_kernel, n, lists), out_shape=jax....  36.4 us
    pallas_call x1, Pallas kernels, shards(): pl.pallas_call(functools.partial(sums_kernel, planes, banks), grid=(plane...  24.2 us
    pallas_call x1, Pallas kernels, shards(): pl.pallas_call(functools.partial(blur_kernel, lists), out_shape=[jax.Shap...  13.2 us
    pallas_call x1, local copies, waits for them, and re-layouts, shards(): pl.pallas_call(functools.partial(reduce_kernel, n, lists), out_shape=jax....  1.72 us

profile of v6, /device:TPU:0, one launch (start us, length us, event | category | flops | bytes accessed | tf_op | source)
XLA Modules:
  0.0 77.1 jit_solution(17042226343678260269)
XLA Ops:
  0.0 0.8 fusion
  0.8 0.1 copy.10
  0.9 0.8 reshape.11.elist
  1.7 13.2 %shard_map.82 = (f32[8,12,64,128]{3,2,1,0:T(8,128)}, f32[3,8,64,128]{3,2,1,0:T(8,128)}, s32[72,128]{1,0:T(8,128)}) custom-call(bf16[3,8,64,128]{3,2,1,0:T(8,128)(2,1)} %affinity.1, f32[3,8,64]{2,1,0:T(8,128)} %scale.1, s32[64,128]{1,0:T(8,128)} %bitcast.3, bf16[4,256,256]{2,1,0:T(8,128)(2,1)} %constant.6.clone.along_y, bf16[4,64,256]{2,1,0:T(8,128)(2,1)} %constant.7.clone.along_z), custom_call_target="tpu_custom_call" | custom-call | tf_op jit(solution)/shard_map/pallas_call | solution.py:372
  14.8 24.2 %shard_map.83.table = f32[4,16,64,128]{3,2,1,0:T(8,128)} custom-call(f32[3,8,64,128]{3,2,1,0:T(8,128)} %get-tuple-element.8.own, f32[8,12,64,128]{3,2,1,0:T(8,128)} %get-tuple-element.9.resp, s32[8,64,128]{2,1,0:T(8,128)} %slots.1, s32[4096]{0:T(1024)} %reshape.11.elist, s32[9216]{0:T(1024)} %bitcast.2), custom_call_target="tpu_custom_call" | custom-call | tf_op jit(solution)/shard_map/pallas_call | solution.py:390
  39.0 36.4 %shard_map.84 = f32[512,64]{1,0:T(8,128)} custom-call(f32[4,16,64,128]{3,2,1,0:T(8,128)} %shard_map.83.table), custom_call_target="tpu_custom_call" | custom-call | tf_op jit(solution)/shard_map/pallas_call | solution.py:409
  75.4 1.7 %copy.11 = f32[512,64]{0,1:T(8,128)} copy(f32[512,64]{1,0:T(8,128)} %shard_map.84) | data formatting | bytes 262144 | tf_op jit(solution)/shard_map/pallas_call | solution.py:409

commit v7 on v6

--- a/solution.py
+++ b/solution.py
@@ -47,7 +47,7 @@
 def orders(n):
     bits = bits_of(n)
     late = bits[:1] + bits[2:] + bits[1:2]
-    return (bits, late, bits, bits)
+    return (bits, late, bits, late)
 
 
 def rank_of(dest, order):
@@ -134,7 +134,7 @@
     dest, inner = home // e_dev, home % e_dev
     half, inner = inner // (parts * tile), inner % (parts * tile)
     part, row = inner // tile, inner % tile
-    rank = jnp.where(part == 1, rank_of(dest, lists[1]), rank_of(dest, lists[0]))
+    rank = jnp.where(part % 2 == 1, rank_of(dest, lists[1]), rank_of(dest, lists[0]))
     place[:rows, :] = ((part * n + rank) * 2 + half) * tile + row
     place[rows:, :] = jnp.full((8, 128), rows * 128, jnp.int32)
 

time: 77.5 us -> 76.4 us (0.986)
  Pallas kernels: 73.8 us -> 72.7 us
    pallas_call x1, Pallas kernels: 36.4 us -> 35.2 us  [shards(): pl.pallas_call(functools.partial(reduce_kernel, n, lists), out_shape=jax....]
where the time goes in v7:
time: 76.4 us; the launch traced here: 76.1 us
  Pallas kernels  72.7 us (95%)
  local copies, waits for them, and re-layouts  2.6 us (3%)
    pallas_call x1, Pallas kernels, shards(): pl.pallas_call(functools.partial(reduce_kernel, n, lists), out_shape=jax....  35.2 us
    pallas_call x1, Pallas kernels, shards(): pl.pallas_call(functools.partial(sums_kernel, planes, banks), grid=(plane...  24.3 us
    pallas_call x1, Pallas kernels, shards(): pl.pallas_call(functools.partial(blur_kernel, lists), out_shape=[jax.Shap...  13.2 us
    pallas_call x1, local copies, waits for them, and re-layouts, shards(): pl.pallas_call(functools.partial(reduce_kernel, n, lists), out_shape=jax....  1.72 us

profile of v7, /device:TPU:0, one launch (start us, length us, event | category | flops | bytes accessed | tf_op | source)
XLA Modules:
  0.0 76.1 jit_solution(12481484742364501021)
XLA Ops:
  0.0 0.8 %fusion = s32[8,64,8]{1,2,0:T(8,128)S(1)} fusion(s32[8,64,8]{1,2,0:T(8,128)} %param.11, s32[8,64]{1,0:T(8,128)} %param.12), kind=kLoop, calls=%fused_computation.1 | loop fusion | flops 8192 | bytes 34816 | tf_op jit(solution)/shard_map/jit(_where)/select_n | solution.py:359
  0.8 0.1 copy.10
  0.9 0.8 reshape.11.elist
  1.7 13.2 %shard_map.82 = (f32[8,12,64,128]{3,2,1,0:T(8,128)}, f32[3,8,64,128]{3,2,1,0:T(8,128)}, s32[72,128]{1,0:T(8,128)}) custom-call(bf16[3,8,64,128]{3,2,1,0:T(8,128)(2,1)} %affinity.1, f32[3,8,64]{2,1,0:T(8,128)} %scale.1, s32[64,128]{1,0:T(8,128)} %bitcast.3, bf16[4,256,256]{2,1,0:T(8,128)(2,1)} %constant.6.clone.along_y, bf16[4,64,256]{2,1,0:T(8,128)(2,1)} %constant.7.clone.along_z), custom_call_target="tpu_custom_call" | custom-call | tf_op jit(solution)/shard_map/pallas_call | solution.py:372
  14.8 24.3 %shard_map.83.table = f32[4,16,64,128]{3,2,1,0:T(8,128)} custom-call(f32[3,8,64,128]{3,2,1,0:T(8,128)} %get-tuple-element.8.own, f32[8,12,64,128]{3,2,1,0:T(8,128)} %get-tuple-element.9.resp, s32[8,64,128]{2,1,0:T(8,128)} %slots.1, s32[4096]{0:T(1024)} %reshape.11.elist, s32[9216]{0:T(1024)} %bitcast.2), custom_call_target="tpu_custom_call" | custom-call | tf_op jit(solution)/shard_map/pallas_call | solution.py:390
  39.1 35.2 %shard_map.84 = f32[512,64]{1,0:T(8,128)} custom-call(f32[4,16,64,128]{3,2,1,0:T(8,128)} %shard_map.83.table), custom_call_target="tpu_custom_call" | custom-call | tf_op jit(solution)/shard_map/pallas_call | solution.py:409
  74.3 1.7 %copy.11 = f32[512,64]{0,1:T(8,128)} copy(f32[512,64]{1,0:T(8,128)} %shard_map.84) | data formatting | bytes 262144 | tf_op jit(solution)/shard_map/pallas_call | solution.py:409

commit v8 on v7

--- a/solution.py
+++ b/solution.py
@@ -287,7 +287,7 @@
     count = n.bit_length() - 1
     recv = scratch[:count]
     acc = scratch[count:2 * count]
-    send_sem, recv_sem = scratch[2 * count:]
+    kept, send_sem, recv_sem, keep_sem = scratch[2 * count:]
     me = lax.axis_index("xy")
     part_id = lax.axis_index("parts")
 
@@ -301,6 +301,10 @@
 
     copies = {}
     lane = lax.broadcasted_iota(jnp.int32, table.shape[2:], 1)
+
+    def keep(p):
+        mine = (me // lists[p][0]) % 2
+        return pltpu.make_async_copy(table.at[p, pl.ds(mine * (n // 2), n // 2)], kept.at[p], keep_sem.at[p])
 
     def start(p, k):
         bit = lists[p][k]
@@ -324,8 +328,13 @@
         mine = (me // bit) % 2
         source = table.at[p] if k == 0 else acc[k - 1].at[p]
         copies[p, k].wait_recv()
+        if k == 0:
+            keep(p).wait()
+            mine_now = kept[p]
+        else:
+            mine_now = source[mine] if size == 1 else source[pl.ds(mine * size, size)]
         if k == count - 1:
-            total = source[mine] + recv[k][p, 0]
+            total = mine_now.reshape(recv[k].shape[2:]) + recv[k][p, 0]
             tile = total.shape[0]
             last = (lane % FEAT) == FEAT - 1
             low = jnp.where(lane < FEAT, total[:, FEAT - 1:FEAT], total[:, 2 * FEAT - 1:])
@@ -334,10 +343,12 @@
             base = (len(lists) + p) * tile
             out[base:base + tile, :] = done[:, FEAT:]
         else:
-            acc[k][p] = source[pl.ds(mine * size, size)] + recv[k][p]
+            acc[k][p] = mine_now.reshape(recv[k].shape[1:]) + recv[k][p]
 
     for p in range(len(lists)):
         start(p, 0)
+    for p in range(len(lists)):
+        keep(p).start()
     for k in range(count):
         for p in range(len(lists)):
             finish(p, k)
@@ -409,11 +420,13 @@
     return pl.pallas_call(
         functools.partial(reduce_kernel, n, lists),
         out_shape=jax.ShapeDtypeStruct((e_dev, FEAT), jnp.float32),
-        in_specs=[whole],
+        in_specs=[pl.BlockSpec(memory_space=pl.ANY)],
         out_specs=whole,
         scratch_shapes=[VMEM((parts, s, tile, 128), jnp.float32) for s in sizes] * 2 + [
+            VMEM((parts, n // 2, tile, 128), jnp.float32),
             pltpu.SemaphoreType.DMA((parts, count)),
             pltpu.SemaphoreType.DMA((parts, count)),
+            pltpu.SemaphoreType.DMA((parts,)),
         ],
         compiler_params=pltpu.CompilerParams(collective_id=0, has_side_effects=True, vmem_limit_bytes=56 << 20),
     )(table)

time: 76.4 us -> 74.9 us (0.980)
  Pallas kernels: 72.7 us -> 71.3 us
    pallas_call x1, Pallas kernels: 35.2 us -> 33.9 us  [shards(): pl.pallas_call(functools.partial(reduce_kernel, n, lists), out_shape=jax....]
where the time goes in v8:
time: 74.9 us; the launch traced here: 74.7 us
  Pallas kernels  71.3 us (95%)
  local copies, waits for them, and re-layouts  2.6 us (3%)
  other arithmetic  0.76 us (1%)
    pallas_call x1, Pallas kernels, shards(): pl.pallas_call(functools.partial(reduce_kernel, n, lists), out_shape=jax....  33.9 us
    pallas_call x1, Pallas kernels, shards(): pl.pallas_call(functools.partial(sums_kernel, planes, banks), grid=(plane...  24.2 us
    pallas_call x1, Pallas kernels, shards(): pl.pallas_call(functools.partial(blur_kernel, lists), out_shape=[jax.Shap...  13.2 us
    pallas_call x1, local copies, waits for them, and re-layouts, shards(): pl.pallas_call(functools.partial(reduce_kernel, n, lists), out_shape=jax....  1.72 us

profile of v8, /device:TPU:0, one launch (start us, length us, event | category | flops | bytes accessed | tf_op | source)
XLA Modules:
  0.0 74.7 jit_solution(10888198873218896898)
XLA Ops:
  0.0 0.8 %fusion = s32[8,64,8]{1,2,0:T(8,128)S(1)} fusion(s32[8,64,8]{1,2,0:T(8,128)} %param.11, s32[8,64]{1,0:T(8,128)} %param.12), kind=kLoop, calls=%fused_computation.1 | loop fusion | flops 8192 | bytes 34816 | tf_op jit(solution)/shard_map/jit(_where)/select_n | solution.py:370
  0.8 0.1 copy.10
  0.9 0.8 %reshape.11.elist = s32[4096]{0:T(1024)} reshape(s32[8,64,8]{2,1,0:T(8,128)S(1)} %copy.10) | data formatting | bytes 32768 | tf_op jit(solution)/shard_map/reshape | solution.py:370
  1.7 13.2 %shard_map.82 = (f32[8,12,64,128]{3,2,1,0:T(8,128)}, f32[3,8,64,128]{3,2,1,0:T(8,128)}, s32[72,128]{1,0:T(8,128)}) custom-call(bf16[3,8,64,128]{3,2,1,0:T(8,128)(2,1)} %affinity.1, f32[3,8,64]{2,1,0:T(8,128)} %scale.1, s32[64,128]{1,0:T(8,128)} %bitcast.3, bf16[4,256,256]{2,1,0:T(8,128)(2,1)} %constant.6.clone.along_y, bf16[4,64,256]{2,1,0:T(8,128)(2,1)} %constant.7.clone.along_z), custom_call_target="tpu_custom_call" | custom-call | tf_op jit(solution)/shard_map/pallas_call | solution.py:383
  14.8 24.2 %shard_map.83.table = f32[4,16,64,128]{3,2,1,0:T(8,128)} custom-call(f32[3,8,64,128]{3,2,1,0:T(8,128)} %get-tuple-element.8.own, f32[8,12,64,128]{3,2,1,0:T(8,128)} %get-tuple-element.9.resp, s32[8,64,128]{2,1,0:T(8,128)} %slots.1, s32[4096]{0:T(1024)} %reshape.11.elist, s32[9216]{0:T(1024)} %bitcast.2), custom_call_target="tpu_custom_call" | custom-call | tf_op jit(solution)/shard_map/pallas_call | solution.py:401
  39.0 33.9 %shard_map.84 = f32[512,64]{1,0:T(8,128)} custom-call(f32[4,16,64,128]{3,2,1,0:T(8,128)} %shard_map.83.table), custom_call_target="tpu_custom_call" | custom-call | tf_op jit(solution)/shard_map/pallas_call | solution.py:420
  72.9 1.7 %copy.11 = f32[512,64]{0,1:T(8,128)} copy(f32[512,64]{1,0:T(8,128)} %shard_map.84) | data formatting | bytes 262144 | tf_op jit(solution)/shard_map/pallas_call | solution.py:420

commit v9 on v8

--- a/solution.py
+++ b/solution.py
@@ -47,7 +47,7 @@
 def orders(n):
     bits = bits_of(n)
     late = bits[:1] + bits[2:] + bits[1:2]
-    return (bits, late, bits, late)
+    return (bits, late) * 4
 
 
 def rank_of(dest, order):

time: 74.9 us -> 79.1 us (1.056)
  Pallas kernels: 71.3 us -> 75.3 us
    pallas_call x1, Pallas kernels: 24.2 us -> 28.5 us  [shards(): pl.pallas_call(functools.partial(sums_kernel, planes, banks), grid=(plane...]
where the time goes in v9:
time: 79.1 us; the launch traced here: 78.7 us
  Pallas kernels  75.3 us (95%)
  local copies, waits for them, and re-layouts  2.6 us (3%)
    pallas_call x1, Pallas kernels, shards(): pl.pallas_call(functools.partial(reduce_kernel, n, lists), out_shape=jax....  33.6 us
    pallas_call x1, Pallas kernels, shards(): pl.pallas_call(functools.partial(sums_kernel, planes, banks), grid=(plane...  28.5 us
    pallas_call x1, Pallas kernels, shards(): pl.pallas_call(functools.partial(blur_kernel, lists), out_shape=[jax.Shap...  13.2 us
    pallas_call x1, local copies, waits for them, and re-layouts, shards(): pl.pallas_call(functools.partial(reduce_kernel, n, lists), out_shape=jax....  1.72 us

profile of v9, /device:TPU:0, one launch (start us, length us, event | category | flops | bytes accessed | tf_op | source)
XLA Modules:
  0.0 78.7 jit_solution(11876447903162988671)
XLA Ops:
  0.0 0.8 fusion
  0.8 0.1 copy.10
  0.9 0.8 reshape.11.elist
  1.7 13.2 %shard_map.82 = (f32[8,12,64,128]{3,2,1,0:T(8,128)}, f32[3,8,64,128]{3,2,1,0:T(8,128)}, s32[72,128]{1,0:T(8,128)}) custom-call(bf16[3,8,64,128]{3,2,1,0:T(8,128)(2,1)} %affinity.1, f32[3,8,64]{2,1,0:T(8,128)} %scale.1, s32[64,128]{1,0:T(8,128)} %bitcast.3, bf16[4,256,256]{2,1,0:T(8,128)(2,1)} %constant.6.clone.along_y, bf16[4,64,256]{2,1,0:T(8,128)(2,1)} %constant.7.clone.along_z), custom_call_target="tpu_custom_call" | custom-call | tf_op jit(solution)/shard_map/pallas_call | solution.py:383
  14.8 28.5 %shard_map.83.table = f32[8,16,32,128]{3,2,1,0:T(8,128)} custom-call(f32[3,8,64,128]{3,2,1,0:T(8,128)} %get-tuple-element.8.own, f32[8,12,64,128]{3,2,1,0:T(8,128)} %get-tuple-element.9.resp, s32[8,64,128]{2,1,0:T(8,128)} %slots.1, s32[4096]{0:T(1024)} %reshape.11.elist, s32[9216]{0:T(1024)} %bitcast.2), custom_call_target="tpu_custom_call" | custom-call | tf_op jit(solution)/shard_map/pallas_call | solution.py:401
  43.4 33.6 %shard_map.84 = f32[512,64]{1,0:T(8,128)} custom-call(f32[8,16,32,128]{3,2,1,0:T(8,128)} %shard_map.83.table), custom_call_target="tpu_custom_call" | custom-call | tf_op jit(solution)/shard_map/pallas_call | solution.py:420
  77.0 1.7 %copy.11 = f32[512,64]{0,1:T(8,128)} copy(f32[512,64]{1,0:T(8,128)} %shard_map.84) | data formatting | bytes 262144 | tf_op jit(solution)/shard_map/pallas_call | solution.py:420
